TPU v7x, 32 devices: a whole 2x2x4 slice. The times are simulated.
32 devices in a mesh: req: 8 (over z, y), exp: 4 (over x, core).
Axes of the slice: x: 2, y: 2, z: 4, core: 2. Of those that a mesh axis runs over, the one named last changes fastest.
Arguments:
- hidden_in: bfloat16 [2048, 2048], P(('req', 'exp')), may hold values from -6 to 6
- query_in: bfloat16 [2048, 2048], P('req', 'exp'), may hold values from -6 to 6
- key_in: bfloat16 [2048, 2048], P('req', 'exp'), may hold values from -6 to 6
- value_in: bfloat16 [2048, 2048], P('req', 'exp'), may hold values from -24 to 24
- query_gain: float32 [128], replicated, may hold values from 0.5 to 2.5
- key_gain: float32 [128], replicated, may hold values from 0.5 to 2.5
- cache_keys: bfloat16 [16, 32, 2048], P('req', None, 'exp'), may hold values from -400 to 400
- cache_values: bfloat16 [16, 32, 2048], P('req', None, 'exp'), may hold values from -24 to 24
- cache_block: int32 [32], replicated, may hold values from -1 to 15, as said below
- request_lengths: int32 [8, 4], P('req'), may hold values from 1 to 128, 256 in all within a row
- out_proj: bfloat16 [2048, 2048], P('exp'), may hold values from -0.125 to 0.125
- norm_gain: float32 [2048], replicated, may hold values from 0.25 to 1.75
- expert_ids: int32 [2048, 8], P(('req', 'exp')), may hold values from 0 to 15, all different within a row; in each aligned block of 64 rows (0 to 63, 64 to 127, ...) at most 40 rows name the same one
- gate_values: float32 [2048, 8], P(('req', 'exp')), may hold values from 0.4 to 1.6
- old_slots: int32 [16], replicated, may hold values from 0 to 15, each once
- new_replicas: int32 [8], replicated, may hold values from 0 to 15
- slot_weights: bfloat16 [16, 3, 2048, 1024], P('req', None, None, 'exp'), may hold values from -0.125 to 0.125
Outputs:
- layer_out: bfloat16 [2048, 2048], P(('req', 'exp'))
- replica_weights: bfloat16 [8, 3, 2048, 1024], P('req', None, None, 'exp')
Inputs may be any that keep to these rules, and one draw needn't show every extreme that they name: `cache_block`: each index of req has exactly 2 of its 4 requests with a block; every block serves exactly one request. `expert_ids`: in each aligned block of 64 rows (the rows of one device) no expert is named by more than 40 rows, a bound that some block reaches; the 8 experts of a row differ. `old_slots`: every expert is in exactly one slot. `request_lengths`: the lengths of each index of req sum to 256.
All inputs are finite; a program needn't handle non-finite values.
Results may differ from a plain program's by a relative error of at most 0.025.
Values may be sent and summed in bfloat16 or wider, within the bound.
No kernel may reach another device: no remote copies, remote signals or barrier semaphores. Data moves between devices by JAX's collectives and lax.ppermute only.
A program may use at most 128 MiB of HBM per device.

v0:
```python
import math

import jax
import jax.numpy as jnp
from jax import lax
from jax.experimental import pallas as pl
from jax.experimental.pallas import tpu as pltpu
from jax.sharding import PartitionSpec as P


def prepare(values, gain, position):
    vector = values.astype(jnp.float32)
    scaled = vector * lax.rsqrt(jnp.mean(vector * vector, axis=-1, keepdims=True) + 1e-06) * gain
    half_size = scaled.shape[-1] // 2
    frequency = 10000.0 ** (-(jnp.arange(half_size, dtype=jnp.float32) * 2.0 / scaled.shape[-1]))
    angles = position[:, None] * frequency[None, :]
    cosine = jnp.cos(angles)[:, None, :]
    sine_part = jnp.sin(angles)[:, None, :]
    lower_half = scaled[..., :half_size]
    upper_half = scaled[..., half_size:]
    rotated = jnp.concatenate(
        [
            lower_half * cosine - upper_half * sine_part,
            upper_half * cosine + lower_half * sine_part,
        ],
        axis=-1,
    )
    return rotated.astype(jnp.bfloat16)


def compact(block_rows, slots_wanted):
    live = block_rows >= 0
    ranks = jnp.cumsum(live.astype(jnp.int32), axis=1) - 1
    request_idx = jnp.arange(block_rows.shape[1], dtype=jnp.int32)[None, :]
    chosen_blocks = []
    chosen_requests = []
    for slot_num in range(slots_wanted):
        picked = live & (ranks == slot_num)
        chosen_blocks.append(jnp.sum(jnp.where(picked, block_rows, 0), axis=1))
        chosen_requests.append(jnp.sum(jnp.where(picked, request_idx, 0), axis=1))
    return (jnp.stack(chosen_blocks, axis=1), jnp.stack(chosen_requests, axis=1))


def experts_kernel(first_slot_ref, tok_ref, weights_ref, out_ref):
    slot_count, _, model_width, _ = weights_ref.shape
    rows = tok_ref[:, :model_width]
    codes = tok_ref[:, model_width:].astype(jnp.float32)
    half_codes = codes.shape[1] // 2
    lane = lax.broadcasted_iota(jnp.int32, codes.shape, 1)
    total = None
    for slot_num in range(slot_count):
        wanted = first_slot_ref[0] + slot_num
        picked = (lane == wanted) | (lane == wanted + half_codes)
        factor = jnp.sum(jnp.where(picked, codes, 0.0), axis=1, keepdims=True)
        gate_act = jnp.dot(rows, weights_ref[slot_num, 0], preferred_element_type=jnp.float32)
        up_act = jnp.dot(rows, weights_ref[slot_num, 1], preferred_element_type=jnp.float32)
        hidden = gate_act / (1.0 + jnp.exp(-gate_act)) * up_act
        hidden = (hidden * factor).astype(jnp.bfloat16)
        part = lax.dot_general(
            hidden,
            weights_ref[slot_num, 2],
            (((1,), (1,)), ((), ())),
            preferred_element_type=jnp.float32,
        )
        total = part if total is None else total + part
    out_ref[...] = total.astype(out_ref.dtype)


def run_experts(first_slot, tokens, slot_weights, block):
    count, ext_width = tokens.shape
    slots_here, mats, width, hidden_size = slot_weights.shape
    return pl.pallas_call(
        experts_kernel,
        out_shape=jax.ShapeDtypeStruct((count, width), jnp.bfloat16),
        grid=(count // block,),
        in_specs=[
            pl.BlockSpec(memory_space=pltpu.SMEM),
            pl.BlockSpec((block, ext_width), lambda i: (i, 0)),
            pl.BlockSpec((slots_here, mats, width, hidden_size), lambda i: (0, 0, 0, 0)),
        ],
        out_specs=pl.BlockSpec((block, width), lambda i: (i, 0)),
        compiler_params=pltpu.CompilerParams(vmem_limit_bytes=40 * 1024 * 1024),
        cost_estimate=pl.CostEstimate(
            flops=2 * count * width * hidden_size * mats * slots_here,
            bytes_accessed=4 * count * width + 2 * slot_weights.size,
            transcendentals=count * hidden_size * slots_here,
        ),
    )(first_slot, tokens, slot_weights)


def turn_pairs(value, step):
    count = lax.axis_size("req")
    return lax.ppermute(value, "req", [(i, (i + 2 * step) % count) for i in range(count)])


def swap(value, mask):
    count = lax.axis_size("req")
    return lax.ppermute(value, "req", [(i, i ^ mask) for i in range(count)])


def after(value, *events):
    return lax.optimization_barrier((value,) + events)[0]


def flip_pair(value):
    count = lax.axis_size("req")
    return lax.ppermute(value, "req", [(i, i ^ 1) for i in range(count)])


def flip_chip(value):
    count = lax.axis_size("exp")
    return lax.ppermute(value, "exp", [(i, i ^ 2) for i in range(count)])


def flip_core(value):
    count = lax.axis_size("exp")
    return lax.ppermute(value, "exp", [(i, i ^ 1) for i in range(count)])


def pick(value, index, axis):
    return lax.dynamic_index_in_dim(value, index, axis, keepdims=False)


def add(first, second):
    return (first.astype(jnp.float32) + second.astype(jnp.float32)).astype(jnp.bfloat16)


def fetch_cache(cache_keys, cache_values, need_blocks):
    me = lax.axis_index("req")
    pair_count = lax.axis_size("req") // 2
    cache_dev = cache_keys.shape[0]
    mine = jnp.stack([cache_keys, cache_values], axis=1)
    column = jnp.stack([mine] + [turn_pairs(mine, step) for step in range(1, pair_count)])
    column = column.reshape((pair_count * cache_dev,) + mine.shape[1:])

    def rows_for(wanted):
        holder = wanted // cache_dev
        back = (me // 2 - holder // 2) % pair_count
        index = back * cache_dev + wanted % cache_dev
        return jnp.stack([pick(column, index[k], 0) for k in range(cache_dev)])

    mine_wanted = pick(need_blocks, me, 0)
    from_pair = flip_pair(rows_for(pick(need_blocks, me ^ 1, 0)))
    here = ((mine_wanted // cache_dev) ^ me) & 1
    return jnp.where((here == 0)[:, None, None, None], rows_for(mine_wanted), from_pair)


def sum_heads(partial_value):
    me = lax.axis_index("exp")
    rows, width = partial_value.shape
    grid = partial_value.reshape(2, 2, rows // 4, width)
    core, chip = me % 2, me // 2
    got = flip_core(pick(grid, 1 - core, 1).astype(jnp.bfloat16))
    level = pick(grid, core, 1) + got.astype(jnp.float32)
    got = flip_chip(pick(level, 1 - chip, 0).astype(jnp.bfloat16))
    return pick(level, chip, 0) + got.astype(jnp.float32)


def spread_tokens(pieces):
    width = pieces[0].shape[1]
    stacked = jnp.stack(pieces)
    cut = stacked.shape[1] // 2
    first, second = stacked[:, :cut], stacked[:, cut:]
    first = jnp.stack([first, flip_pair(first)])
    second = jnp.stack([second, flip_chip(second)])
    first_far, second_far = flip_chip(first), flip_pair(second)
    parts = [first, first_far, second, second_far]
    return jnp.concatenate([part.reshape(-1, width) for part in parts])


def gather_sums(total, piece_count):
    rows, width = total.shape
    cut = rows // (8 * piece_count)
    first, second = total.reshape(2, 2, 2, piece_count, cut, width)
    first = add(first[0], flip_chip(first[1]))
    second = add(second[0], flip_pair(second[1]))
    first = add(first[0], flip_pair(first[1]))
    second = add(second[0], flip_chip(second[1]))
    return jnp.concatenate([first, second], axis=1)


def mix(normed, codes, slot_weights, events):
    pair_count = lax.axis_size("req") // 2
    first_slot = (lax.axis_index("req") * slot_weights.shape[0]).astype(jnp.int32).reshape(1)
    ext = jnp.concatenate([normed, codes], axis=1)
    pieces = [ext] + [turn_pairs(ext, step) for step in range(1, pair_count)]
    events["spread"] = pieces[1:]
    total = None
    for begin in range(0, pair_count, 2):
        here = spread_tokens(pieces[begin : begin + 2])
        events["gathered"] = [here]
        there = flip_core(here)
        far_mixed = run_experts(first_slot, there, slot_weights, 256)
        back = flip_core(far_mixed)
        mixed = run_experts(first_slot, here, slot_weights, 256)
        events["mixed"] = [mixed, far_mixed]
        sums = gather_sums(add(mixed, back), 2)
        for offset in range(2):
            step = begin + offset
            part = sums[offset] if step == 0 else turn_pairs(sums[offset], -step)
            part = part.astype(jnp.float32)
            total = part if total is None else total + part
    return total


def spread_weights(slot_weights, event):
    me = lax.axis_index("req")
    half = lax.axis_size("req") // 2
    spot = me % half
    slots_here = slot_weights.shape[0]
    chunks = slot_weights.reshape(slots_here, half, -1, slot_weights.shape[-1])
    held = [pick(chunks, spot, 1)]
    for mask in range(1, half):
        source = chunks if mask < 3 else after(chunks, event)
        held.append(swap(pick(source, spot ^ mask, 1), mask))
    return jnp.concatenate(held)


def collect_replicas(held, source_slot, slots_here, events):
    me = lax.axis_index("req")
    count = lax.axis_size("req")
    half = count // 2
    spot = me % half
    arrived = {}
    order = [half + mask for mask in range(half)] + list(range(half))
    for place, mask in enumerate(order):
        source = held
        if place < 2 or mask == 1:
            source = after(held, *events["spread"])
        elif place == 2:
            source = after(held, *events["gathered"])
        elif mask:
            source = after(held, *events["mixed"])
        slot = pick(source_slot, me ^ mask, 0)
        index = (spot ^ (slot // slots_here % half)) * slots_here + slot % slots_here
        piece = pick(source, index, 0)
        arrived[mask] = swap(piece, mask) if mask else piece
    same = pick(source_slot, me, 0) // slots_here // half == me // half
    result = jnp.zeros((half,) + held.shape[1:], held.dtype)
    for mask in range(half):
        piece = jnp.where(same, arrived[mask], arrived[half + mask])
        result = lax.dynamic_update_index_in_dim(result, piece, spot ^ mask, 0)
    return result


def body(
    hidden_in,
    query_in,
    key_in,
    value_in,
    query_gain,
    key_gain,
    cache_keys,
    cache_values,
    cache_block,
    request_lengths,
    out_proj,
    norm_gain,
    expert_ids,
    gate_values,
    old_slots,
    new_replicas,
    slot_weights,
):
    req_count = lax.axis_size("req")
    exp_count = lax.axis_size("exp")
    group_idx = lax.axis_index("req")
    tok_grp, width_q = query_in.shape
    tok_dev, model_width = hidden_in.shape
    head_size = query_gain.shape[0]
    head_count = width_q // head_size
    cache_dev = cache_keys.shape[0]
    pre_len = cache_keys.shape[1]
    req_grp = request_lengths.shape[1]
    lengths = request_lengths[0]
    req_ends = jnp.cumsum(lengths)
    starts = req_ends - lengths
    places = jnp.arange(tok_grp, dtype=jnp.int32)
    member = (places[:, None] >= starts[None, :]) & (places[:, None] < req_ends[None, :])
    request_idx = jnp.arange(req_grp, dtype=jnp.int32)
    segment = jnp.sum(jnp.where(member, request_idx[None, :], 0), axis=1)
    offset = places - jnp.sum(jnp.where(member, starts[None, :], 0), axis=1)
    block_rows = cache_block.reshape(req_count, req_grp)
    my_blocks = lax.dynamic_index_in_dim(block_rows, group_idx, 0, keepdims=False)
    has_cache = my_blocks >= 0
    token_cached = jnp.sum(jnp.where(member & has_cache[None, :], 1, 0), axis=1) > 0
    position = (offset + jnp.where(token_cached, pre_len, 0)).astype(jnp.float32)
    need_blocks, need_requests = compact(block_rows, cache_dev)
    my_requests = lax.dynamic_index_in_dim(need_requests, group_idx, 0, keepdims=False)
    far_cache = fetch_cache(cache_keys, cache_values, need_blocks)
    far_keys, far_values = far_cache[:, 0], far_cache[:, 1]
    held = spread_weights(slot_weights, far_cache)
    query_n = prepare(query_in.reshape(tok_grp, head_count, head_size), query_gain, position)
    key_n = prepare(key_in.reshape(tok_grp, head_count, head_size), key_gain, position)
    keyset = jnp.concatenate(
        [key_n, far_keys.reshape(cache_dev * pre_len, head_count, head_size)], axis=0
    )
    valueset = jnp.concatenate(
        [
            value_in.reshape(tok_grp, head_count, head_size),
            far_values.reshape(cache_dev * pre_len, head_count, head_size),
        ],
        axis=0,
    )
    key_request = jnp.concatenate([segment, jnp.repeat(my_requests, pre_len)])
    allowed = segment[:, None] == key_request[None, :]
    scores = jnp.einsum("qhd,khd->hqk", query_n, keyset, preferred_element_type=jnp.float32) * (
        1.0 / math.sqrt(head_size)
    )
    scores = jnp.where(allowed[None], scores, -1e30)
    peak = jnp.max(scores, axis=-1, keepdims=True)
    expos = jnp.exp(scores - peak)
    weights = (expos / jnp.sum(expos, axis=-1, keepdims=True)).astype(jnp.bfloat16)
    attended = jnp.einsum("hqk,khd->qhd", weights, valueset, preferred_element_type=jnp.float32)
    attended = attended.astype(jnp.bfloat16).reshape(tok_grp, width_q)
    attn_out = sum_heads(jnp.dot(attended, out_proj, preferred_element_type=jnp.float32))
    residual = hidden_in.astype(jnp.float32) + attn_out
    normed = (
        residual
        * lax.rsqrt(jnp.mean(residual * residual, axis=-1, keepdims=True) + 1e-06)
        * norm_gain
    ).astype(jnp.bfloat16)
    slot_total = old_slots.shape[0]
    slot_range = jnp.arange(slot_total, dtype=jnp.int32)
    slot_of = jnp.sum(
        jnp.where(old_slots[None, :] == slot_range[:, None], slot_range[None, :], 0), axis=1
    )
    dense_gates = jnp.sum(
        jnp.where(expert_ids[:, :, None] == old_slots[None, None, :], gate_values[:, :, None], 0.0),
        axis=1,
    )
    high_part = dense_gates.astype(jnp.bfloat16)
    low_part = (dense_gates - high_part.astype(jnp.float32)).astype(jnp.bfloat16)
    lanes = max(64, slot_total)
    gap = ((0, 0), (0, lanes - slot_total))
    codes = jnp.concatenate([jnp.pad(high_part, gap), jnp.pad(low_part, gap)], axis=1)
    events = {}
    mixture = mix(normed, codes, slot_weights, events)
    layer_out = (residual + mixture).astype(jnp.bfloat16)
    replica_onehot = new_replicas[:, None] == slot_range[None, :]
    source_slot = jnp.sum(jnp.where(replica_onehot, slot_of[None, :], 0), axis=1)
    replica_weights = collect_replicas(held, source_slot, slot_weights.shape[0], events)
    return (layer_out, replica_weights.reshape((1,) + slot_weights.shape[1:]))


def solution(mesh):
    in_specs = (
        P(("req", "exp"), None),
        P("req", "exp"),
        P("req", "exp"),
        P("req", "exp"),
        P(),
        P(),
        P("req", None, "exp"),
        P("req", None, "exp"),
        P(),
        P("req", None),
        P("exp", None),
        P(),
        P(("req", "exp"), None),
        P(("req", "exp"), None),
        P(),
        P(),
        P("req", None, None, "exp"),
    )
    out_specs = (P(("req", "exp"), None), P("req", None, None, "exp"))
    return jax.shard_map(body, mesh=mesh, in_specs=in_specs, out_specs=out_specs, check_vma=False)
```

profile of v0, /device:TPU:0, one launch (start us, length us, event | category | flops | bytes accessed | tf_op | source)
XLA Modules:
  0.0 372.1 jit_solution(12843004745108631670)
XLA Ops:
  0.7 1.7 fusion.69
  2.4 5.0 %collective-permute-start.2 = (bf16[2,2,32,512]{3,2,1,0:T(8,128)(2,1)}, bf16[2,2,32,512]{3,2,1,0:T(8,128)(2,1)}, u32[]{:S(2)}, u32[]{:S(2)}) collective-permute-start(bf16[2,2,32,512]{3,2,1,0:T(8,128)(2,1)} %get-tuple-element.63), channel_id=1, source_target_pairs={{0,24},{4,28},{8,0},{12,4},{16,8},{20,12},{24,16},{28,20},{1,25},{... | collective-permute-start | bytes 393224 | tf_op jit(solution)/shard_map/ppermute | solution.py:93
  30.5 1.6 collective-permute-start.3
  32.2 3.3 collective-permute-done.3
  35.8 3.3 fusion.78
  39.1 1.7 fusion.6
  43.3 4.8 %dynamic-slice_bitcast_fusion.3 = (bf16[2,1536,256]{2,1,0:T(8,128)(2,1)}, bf16[2,1536,256]{2,1,0:T(8,128)(2,1)}, bf16[2,1536,256]{2,1,0:T(8,128)(2,1)}) fusion(bf16[2,4,1536,256]{3,2,1,0:T(8,128)(2,1)} %bitcast.172, s32[]{:T(128)S(6)} %select_n.367, s32[]{:T(128)S(6)} %select_n.369, s32[]{:T(128)S(6)} %select_n.368), kind=kLoop, calls=%fused_computation.12 | loop fusion | bytes 9437196 | tf_op jit(solution)/shard_map/jit(dynamic_index_in_dim)/squeeze | solution.py:121
  48.0 2.5 collective-permute-start.33
  50.5 1.5 collective-permute-start.32
  53.4 1.6 collective-permute-start.5
  79.3 1.5 collective-permute-start.19
  80.8 1.5 dynamic-slice_bitcast_fusion
  82.8 12.0 %collective-permute-done.18 = bf16[64,2176]{1,0:T(8,128)(2,1)S(1)} collective-permute-done((bf16[64,2176]{1,0:T(8,128)(2,1)S(1)}, bf16[64,2176]{1,0:T(8,128)(2,1)S(1)}, u32[]{:S(2)}, u32[]{:S(2)}) %collective-permute-start.18) | collective-permute-done | bytes 278560 | tf_op jit(solution)/shard_map/ppermute | solution.py:93
  94.8 3.1 collective-permute-done.19
  98.0 1.6 collective-permute-start.22
  99.5 38.5 %collective-permute-done.6 = bf16[64,2176]{1,0:T(8,128)(2,1)S(1)} collective-permute-done((bf16[64,2176]{1,0:T(8,128)(2,1)S(1)}, bf16[64,2176]{1,0:T(8,128)(2,1)S(1)}, u32[]{:S(2)}, u32[]{:S(2)}) %collective-permute-start.6) | collective-permute-done | bytes 278560 | tf_op jit(solution)/shard_map/ppermute | solution.py:93
  138.0 1.5 collective-permute-start.20
  139.6 1.5 collective-permute-start.9
  141.2 5.1 %collective-permute-done.20 = bf16[2,32,2176]{2,1,0:T(8,128)(2,1)S(1)} collective-permute-done((bf16[2,32,2176]{2,1,0:T(8,128)(2,1)S(1)}, bf16[2,32,2176]{2,1,0:T(8,128)(2,1)S(1)}, u32[]{:S(2)}, u32[]{:S(2)}) %collective-permute-start.20) | collective-permute-done | bytes 278560 | tf_op jit(solution)/shard_map/ppermute | solution.py:107
  146.3 1.5 collective-permute-start.7
  148.4 7.4 %collective-permute-done.7 = bf16[2,32,2176]{2,1,0:T(8,128)(2,1)S(1)} collective-permute-done((bf16[2,32,2176]{2,1,0:T(8,128)(2,1)S(1)}, bf16[2,32,2176]{2,1,0:T(8,128)(2,1)S(1)}, u32[]{:S(2)}, u32[]{:S(2)}) %collective-permute-start.7) | collective-permute-done | bytes 278560 | tf_op jit(solution)/shard_map/ppermute | solution.py:107
  157.5 8.1 %collective-permute-done.23 = bf16[2,2,32,2176]{3,2,1,0:T(8,128)(2,1)S(1)} collective-permute-done((bf16[2,2,32,2176]{3,2,1,0:T(8,128)(2,1)S(1)}, bf16[2,2,32,2176]{3,2,1,0:T(8,128)(2,1)S(1)}, u32[]{:S(2)}, u32[]{:S(2)}) %collective-permute-start.23) | collective-permute-done | bytes 557088 | tf_op jit(solution)/shard_map/ppermute | solution.py:107
  165.5 1.5 collective-permute-start.10
  168.8 3.7 pad_maximum_fusion
  172.6 5.4 %collective-permute-done.10 = bf16[2,2,32,2176]{3,2,1,0:T(8,128)(2,1)S(1)} collective-permute-done((bf16[2,2,32,2176]{3,2,1,0:T(8,128)(2,1)S(1)}, bf16[2,2,32,2176]{3,2,1,0:T(8,128)(2,1)S(1)}, u32[]{:S(2)}, u32[]{:S(2)}) %collective-permute-start.10) | collective-permute-done | bytes 557088 | tf_op jit(solution)/shard_map/ppermute | solution.py:107
  181.3 3.9 %collective-permute-start.37 = (bf16[1536,256]{1,0:T(8,128)(2,1)}, bf16[1536,256]{1,0:T(8,128)(2,1)}, u32[]{:S(2)}, u32[]{:S(2)}) collective-permute-start(bf16[1536,256]{1,0:T(8,128)(2,1)} %get-tuple-element.30), channel_id=1, source_target_pairs={{0,20},{4,16},{8,28},{12,24},{16,4},{20,0},{24,12},{28,8},{1,21},{... | collective-permute-start | bytes 2359304 | tf_op jit(solution)/shard_map/ppermute | solution.py:98
  185.2 3.8 %shard_map.178 = bf16[512,2048]{1,0:T(8,128)(2,1)S(1)} custom-call(s32[1]{0:T(128)} %bitcast.32.first_slot_ref, bf16[512,2176]{1,0:T(8,128)(2,1)S(1)} %pad_maximum_fusion.2.tok_ref, bf16[2,3,2048,256]{3,2,1,0:T(8,128)(2,1)S(1)} %bitcast.175), custom_call_target="tpu_custom_call" | custom-call | flops 3221225472 | bytes 10485760 | tf_op jit(solution)/shard_map/pallas_call | solution.py:72
  190.2 3.8 %shard_map.176 = bf16[512,2048]{1,0:T(8,128)(2,1)S(1)} custom-call(s32[1]{0:T(128)} %bitcast.32.first_slot_ref, bf16[512,2176]{1,0:T(8,128)(2,1)S(1)} %pad_maximum_fusion.1.tok_ref, bf16[2,3,2048,256]{3,2,1,0:T(8,128)(2,1)S(1)} %bitcast.175), custom_call_target="tpu_custom_call" | custom-call | flops 3221225472 | bytes 10485760 | tf_op jit(solution)/shard_map/pallas_call | solution.py:72
  195.5 3.8 %shard_map.179 = bf16[512,2048]{1,0:T(8,128)(2,1)S(1)} custom-call(s32[1]{0:T(128)} %bitcast.32.first_slot_ref, bf16[512,2176]{1,0:T(8,128)(2,1)S(1)} %collective-permute-done.24.tok_ref, bf16[2,3,2048,256]{3,2,1,0:T(8,128)(2,1)S(1)} %bitcast.175), custom_call_target="tpu_custom_call" | custom-call | flops 3221225472 | bytes 10485760 | tf_op jit(solution)/shard_map/pallas_call | solution.py:72
  199.4 53.2 %collective-permute-done.35 = bf16[1536,256]{1,0:T(8,128)(2,1)S(1)} collective-permute-done((bf16[1536,256]{1,0:T(8,128)(2,1)S(1)}, bf16[1536,256]{1,0:T(8,128)(2,1)S(1)}, u32[]{:S(2)}, u32[]{:S(2)}) %collective-permute-start.35) | collective-permute-done | bytes 786464 | tf_op jit(solution)/shard_map/ppermute | solution.py:98
  255.9 3.2 dynamic-slice_bitcast_fusion.4
  259.1 3.8 %shard_map.177 = bf16[512,2048]{1,0:T(8,128)(2,1)S(1)} custom-call(s32[1]{0:T(128)} %bitcast.32.first_slot_ref, bf16[512,2176]{1,0:T(8,128)(2,1)S(1)} %collective-permute-done.11.tok_ref, bf16[2,3,2048,256]{3,2,1,0:T(8,128)(2,1)S(1)} %bitcast.175), custom_call_target="tpu_custom_call" | custom-call | flops 3221225472 | bytes 10485760 | tf_op jit(solution)/shard_map/pallas_call | solution.py:72
  263.5 6.0 %collective-permute-done.37 = bf16[1536,256]{1,0:T(8,128)(2,1)} collective-permute-done((bf16[1536,256]{1,0:T(8,128)(2,1)}, bf16[1536,256]{1,0:T(8,128)(2,1)}, u32[]{:S(2)}, u32[]{:S(2)}) %collective-permute-start.37) | collective-permute-done | bytes 786464 | tf_op jit(solution)/shard_map/ppermute | solution.py:98
  271.0 1.9 collective-permute-start.41
  272.9 13.0 %collective-permute-done.38 = bf16[1536,256]{1,0:T(8,128)(2,1)S(1)} collective-permute-done((bf16[1536,256]{1,0:T(8,128)(2,1)}, bf16[1536,256]{1,0:T(8,128)(2,1)S(1)}, u32[]{:S(2)}, u32[]{:S(2)}) %collective-permute-start.38) | collective-permute-done | bytes 786464 | tf_op jit(solution)/shard_map/ppermute | solution.py:98
  286.1 2.5 add_convert_fusion
  288.8 1.5 collective-permute-start.26
  291.9 1.6 collective-permute-start.15
  293.5 9.3 %collective-permute-done.26 = bf16[2,2,32,2048]{3,2,1,0:T(8,128)(2,1)S(1)} collective-permute-done((bf16[2,2,32,2048]{3,2,1,0:T(8,128)(2,1)S(1)}, bf16[2,2,32,2048]{3,2,1,0:T(8,128)(2,1)S(1)}, u32[]{:S(2)}, u32[]{:S(2)}) %collective-permute-start.26) | collective-permute-done | bytes 524320 | tf_op jit(solution)/shard_map/ppermute | solution.py:112
  304.4 26.5 %collective-permute-done.28 = bf16[2,2,32,2048]{3,2,1,0:T(8,128)(2,1)S(1)} collective-permute-done((bf16[2,2,32,2048]{3,2,1,0:T(8,128)(2,1)S(1)}, bf16[2,2,32,2048]{3,2,1,0:T(8,128)(2,1)S(1)}, u32[]{:S(2)}, u32[]{:S(2)}) %collective-permute-start.28) | collective-permute-done | bytes 524320 | tf_op jit(solution)/shard_map/ppermute | solution.py:107
  330.9 1.5 collective-permute-start.27
  332.5 9.6 %collective-permute-done.15 = bf16[2,2,32,2048]{3,2,1,0:T(8,128)(2,1)S(1)} collective-permute-done((bf16[2,2,32,2048]{3,2,1,0:T(8,128)(2,1)S(1)}, bf16[2,2,32,2048]{3,2,1,0:T(8,128)(2,1)S(1)}, u32[]{:S(2)}, u32[]{:S(2)}) %collective-permute-start.15) | collective-permute-done | bytes 524320 | tf_op jit(solution)/shard_map/ppermute | solution.py:107
  344.5 3.1 collective-permute-done.27
  347.6 1.5 collective-permute-start.14
  349.2 2.1 collective-permute-done.29
  351.5 4.4 %collective-permute-done.16 = bf16[2,32,2048]{2,1,0:T(8,128)(2,1)S(1)} collective-permute-done((bf16[2,32,2048]{2,1,0:T(8,128)(2,1)S(1)}, bf16[2,32,2048]{2,1,0:T(8,128)(2,1)S(1)}, u32[]{:S(2)}, u32[]{:S(2)}) %collective-permute-start.16) | collective-permute-done | bytes 262176 | tf_op jit(solution)/shard_map/ppermute | solution.py:112
  357.5 4.9 %collective-permute-done.31 = bf16[64,2048]{1,0:T(8,128)(2,1)S(1)} collective-permute-done((bf16[64,2048]{1,0:T(8,128)(2,1)S(1)}, bf16[64,2048]{1,0:T(8,128)(2,1)S(1)}, u32[]{:S(2)}, u32[]{:S(2)}) %collective-permute-start.31) | collective-permute-done | bytes 262176 | tf_op jit(solution)/shard_map/ppermute | solution.py:93
  362.4 8.6 %collective-permute-done.30 = bf16[64,2048]{1,0:T(8,128)(2,1)S(1)} collective-permute-done((bf16[64,2048]{1,0:T(8,128)(2,1)S(1)}, bf16[64,2048]{1,0:T(8,128)(2,1)S(1)}, u32[]{:S(2)}, u32[]{:S(2)}) %collective-permute-start.30) | collective-permute-done | bytes 262176 | tf_op jit(solution)/shard_map/ppermute | solution.py:93
  (194 shorter events, 48.0 us)
Async XLA Ops:
  0.6 40.4 %copy-start = (bf16[512,2048]{1,0:T(8,128)(2,1)S(1)}, bf16[512,2048]{1,0:T(8,128)(2,1)}, u32[]{:S(2)}) copy-start(bf16[512,2048]{1,0:T(8,128)(2,1)} %param.27) | copy-start | bytes 6291460
  2.4 27.0 %collective-permute-start.2 = (bf16[2,2,32,512]{3,2,1,0:T(8,128)(2,1)}, bf16[2,2,32,512]{3,2,1,0:T(8,128)(2,1)}, u32[]{:S(2)}, u32[]{:S(2)}) collective-permute-start(bf16[2,2,32,512]{3,2,1,0:T(8,128)(2,1)} %get-tuple-element.63), channel_id=1, source_target_pairs={{0,24},{4,28},{8,0},{12,4},{16,8},{20,12},{24,16},{28,20},{1,25},{... | collective-permute-start | bytes 393224 | tf_op jit(solution)/shard_map/ppermute | solution.py:93
  7.4 21.9 %collective-permute-start.1 = (bf16[2,2,32,512]{3,2,1,0:T(8,128)(2,1)}, bf16[2,2,32,512]{3,2,1,0:T(8,128)(2,1)}, u32[]{:S(2)}, u32[]{:S(2)}) collective-permute-start(bf16[2,2,32,512]{3,2,1,0:T(8,128)(2,1)} %get-tuple-element.63), channel_id=1, source_target_pairs={{0,16},{4,20},{8,24},{12,28},{16,0},{20,4},{24,8},{28,12},{1,17},{... | collective-permute-start | bytes 393224 | tf_op jit(solution)/shard_map/ppermute | solution.py:93
  7.4 21.9 %collective-permute-start = (bf16[2,2,32,512]{3,2,1,0:T(8,128)(2,1)}, bf16[2,2,32,512]{3,2,1,0:T(8,128)(2,1)}, u32[]{:S(2)}, u32[]{:S(2)}) collective-permute-start(bf16[2,2,32,512]{3,2,1,0:T(8,128)(2,1)} %get-tuple-element.63), channel_id=1, source_target_pairs={{0,8},{4,12},{8,16},{12,20},{16,24},{20,28},{24,0},{28,4},{1,9},{5... | collective-permute-start | bytes 393224 | tf_op jit(solution)/shard_map/ppermute | solution.py:93
  30.5 5.0 %collective-permute-start.3 = (bf16[2,2,32,512]{3,2,1,0:T(8,128)(2,1)S(1)}, bf16[2,2,32,512]{3,2,1,0:T(8,128)(2,1)S(1)}, u32[]{:S(2)}, u32[]{:S(2)}) collective-permute-start(bf16[2,2,32,512]{3,2,1,0:T(8,128)(2,1)S(1)} %pad_maximum_fusion.13), channel_id=1, source_target_pairs={{0,4},{4,0},{8,12},{12,8},{16,20},{20,16},{24,28},{28,24},{1,5},{5... | collective-permute-start | bytes 393224 | tf_op jit(solution)/shard_map/ppermute | solution.py:107
  43.1 9.1 %collective-permute-start.4 = (bf16[2,64,2048]{2,1,0:T(8,128)(2,1)S(1)}, bf16[2,64,2048]{2,1,0:T(8,128)(2,1)S(1)}, u32[]{:S(2)}, u32[]{:S(2)}) collective-permute-start(bf16[2,64,2048]{2,1,0:T(8,128)(2,1)S(1)} %fusion.11), channel_id=1, source_target_pairs={{0,1},{1,0},{2,3},{3,2},{4,5},{5,4},{6,7},{7,6},{8,9},{9,8},{10,11... | collective-permute-start | bytes 1572872 | tf_op jit(solution)/shard_map/ppermute | solution.py:117
  48.0 28.8 %copy-start.14 = (bf16[64,2048]{1,0:T(8,128)(2,1)S(1)}, bf16[64,2048]{1,0:T(8,128)(2,1)}, u32[]{:S(2)}) copy-start(bf16[64,2048]{1,0:T(8,128)(2,1)} %param.17) | copy-start | bytes 786436
  48.0 120.7 %collective-permute-start.33 = (bf16[2,1536,256]{2,1,0:T(8,128)(2,1)}, bf16[2,1536,256]{2,1,0:T(8,128)(2,1)}, u32[]{:S(2)}, u32[]{:S(2)}) collective-permute-start(bf16[2,1536,256]{2,1,0:T(8,128)(2,1)} %get-tuple-element.34), channel_id=1, source_target_pairs={{0,8},{4,12},{8,0},{12,4},{16,24},{20,28},{24,16},{28,20},{1,9},{5... | collective-permute-start | bytes 4718600 | tf_op jit(solution)/shard_map/ppermute | solution.py:98
  50.5 118.3 %collective-permute-start.32 = (bf16[2,1536,256]{2,1,0:T(8,128)(2,1)}, bf16[2,1536,256]{2,1,0:T(8,128)(2,1)}, u32[]{:S(2)}, u32[]{:S(2)}) collective-permute-start(bf16[2,1536,256]{2,1,0:T(8,128)(2,1)} %get-tuple-element.35), channel_id=1, source_target_pairs={{0,4},{4,0},{8,12},{12,8},{16,20},{20,16},{24,28},{28,24},{1,5},{5... | collective-permute-start | bytes 4718600 | tf_op jit(solution)/shard_map/ppermute | solution.py:98
  52.2 25.8 %copy-start.15 = (f32[2048]{0:T(1024)S(1)}, f32[2048]{0:T(1024)}, u32[]{:S(2)}) copy-start(f32[2048]{0:T(1024)} %param.28) | copy-start | bytes 24580
  53.4 23.4 %collective-permute-start.5 = (bf16[64,2048]{1,0:T(8,128)(2,1)S(1)}, bf16[64,2048]{1,0:T(8,128)(2,1)S(1)}, u32[]{:S(2)}, u32[]{:S(2)}) collective-permute-start(bf16[64,2048]{1,0:T(8,128)(2,1)S(1)} %fusion.31), channel_id=1, source_target_pairs={{0,2},{1,3},{2,0},{3,1},{4,6},{5,7},{6,4},{7,5},{8,10},{9,11},{10,... | collective-permute-start | bytes 786440 | tf_op jit(solution)/shard_map/ppermute | solution.py:112
  78.3 16.5 %collective-permute-start.18 = (bf16[64,2176]{1,0:T(8,128)(2,1)S(1)}, bf16[64,2176]{1,0:T(8,128)(2,1)S(1)}, u32[]{:S(2)}, u32[]{:S(2)}) collective-permute-start(bf16[64,2176]{1,0:T(8,128)(2,1)S(1)} %concatenate.40), channel_id=1, source_target_pairs={{0,16},{4,20},{8,24},{12,28},{16,0},{20,4},{24,8},{28,12},{1,17},{... | collective-permute-start | bytes 835592 | tf_op jit(solution)/shard_map/ppermute | solution.py:93
  79.3 18.6 %collective-permute-start.19 = (bf16[64,2176]{1,0:T(8,128)(2,1)S(1)}, bf16[64,2176]{1,0:T(8,128)(2,1)S(1)}, u32[]{:S(2)}, u32[]{:S(2)}) collective-permute-start(bf16[64,2176]{1,0:T(8,128)(2,1)S(1)} %concatenate.40), channel_id=1, source_target_pairs={{0,24},{4,28},{8,0},{12,4},{16,8},{20,12},{24,16},{28,20},{1,25},{... | collective-permute-start | bytes 835592 | tf_op jit(solution)/shard_map/ppermute | solution.py:93
  82.3 86.5 %collective-permute-start.34 = (bf16[2,1536,256]{2,1,0:T(8,128)(2,1)S(1)}, bf16[2,1536,256]{2,1,0:T(8,128)(2,1)S(1)}, u32[]{:S(2)}, u32[]{:S(2)}) collective-permute-start(bf16[2,1536,256]{2,1,0:T(8,128)(2,1)S(1)} %dynamic-slice_bitcast_fusion), channel_id=1, source_target_pairs={{0,12},{4,8},{8,4},{12,0},{16,28},{20,24},{24,20},{28,16},{1,13},{... | collective-permute-start | bytes 4718600 | tf_op jit(solution)/shard_map/ppermute | solution.py:98
  94.8 43.2 %collective-permute-start.6 = (bf16[64,2176]{1,0:T(8,128)(2,1)S(1)}, bf16[64,2176]{1,0:T(8,128)(2,1)S(1)}, u32[]{:S(2)}, u32[]{:S(2)}) collective-permute-start(bf16[64,2176]{1,0:T(8,128)(2,1)S(1)} %concatenate.40), channel_id=1, source_target_pairs={{0,8},{4,12},{8,16},{12,20},{16,24},{20,28},{24,0},{28,4},{1,9},{5... | collective-permute-start | bytes 835592 | tf_op jit(solution)/shard_map/ppermute | solution.py:93
  98.0 41.6 %collective-permute-start.22 = (bf16[2,32,2176]{2,1,0:T(8,128)(2,1)S(1)}, bf16[2,32,2176]{2,1,0:T(8,128)(2,1)S(1)}, u32[]{:S(2)}, u32[]{:S(2)}) collective-permute-start(bf16[2,32,2176]{2,1,0:T(8,128)(2,1)S(1)} %get-tuple-element.51), channel_id=1, source_target_pairs={{0,2},{1,3},{2,0},{3,1},{4,6},{5,7},{6,4},{7,5},{8,10},{9,11},{10,... | collective-permute-start | bytes 835592 | tf_op jit(solution)/shard_map/ppermute | solution.py:112
  138.0 8.2 %collective-permute-start.20 = (bf16[2,32,2176]{2,1,0:T(8,128)(2,1)S(1)}, bf16[2,32,2176]{2,1,0:T(8,128)(2,1)S(1)}, u32[]{:S(2)}, u32[]{:S(2)}) collective-permute-start(bf16[2,32,2176]{2,1,0:T(8,128)(2,1)S(1)} %get-tuple-element.50), channel_id=1, source_target_pairs={{0,4},{4,0},{8,12},{12,8},{16,20},{20,16},{24,28},{28,24},{1,5},{5... | collective-permute-start | bytes 835592 | tf_op jit(solution)/shard_map/ppermute | solution.py:107
  139.6 8.3 %collective-permute-start.9 = (bf16[2,32,2176]{2,1,0:T(8,128)(2,1)S(1)}, bf16[2,32,2176]{2,1,0:T(8,128)(2,1)S(1)}, u32[]{:S(2)}, u32[]{:S(2)}) collective-permute-start(bf16[2,32,2176]{2,1,0:T(8,128)(2,1)S(1)} %get-tuple-element.49), channel_id=1, source_target_pairs={{0,2},{1,3},{2,0},{3,1},{4,6},{5,7},{6,4},{7,5},{8,10},{9,11},{10,... | collective-permute-start | bytes 835592 | tf_op jit(solution)/shard_map/ppermute | solution.py:112
  146.3 9.6 %collective-permute-start.7 = (bf16[2,32,2176]{2,1,0:T(8,128)(2,1)S(1)}, bf16[2,32,2176]{2,1,0:T(8,128)(2,1)S(1)}, u32[]{:S(2)}, u32[]{:S(2)}) collective-permute-start(bf16[2,32,2176]{2,1,0:T(8,128)(2,1)S(1)} %get-tuple-element.48), channel_id=1, source_target_pairs={{0,4},{4,0},{8,12},{12,8},{16,20},{20,16},{24,28},{28,24},{1,5},{5... | collective-permute-start | bytes 835592 | tf_op jit(solution)/shard_map/ppermute | solution.py:107
  147.9 17.7 %collective-permute-start.23 = (bf16[2,2,32,2176]{3,2,1,0:T(8,128)(2,1)S(1)}, bf16[2,2,32,2176]{3,2,1,0:T(8,128)(2,1)S(1)}, u32[]{:S(2)}, u32[]{:S(2)}) collective-permute-start(bf16[2,2,32,2176]{3,2,1,0:T(8,128)(2,1)S(1)} %pad_maximum_fusion.6), channel_id=1, source_target_pairs={{0,4},{4,0},{8,12},{12,8},{16,20},{20,16},{24,28},{28,24},{1,5},{5... | collective-permute-start | bytes 1671176 | tf_op jit(solution)/shard_map/ppermute | solution.py:107
  155.9 11.2 %collective-permute-start.21 = (bf16[2,2,32,2176]{3,2,1,0:T(8,128)(2,1)S(1)}, bf16[2,2,32,2176]{3,2,1,0:T(8,128)(2,1)S(1)}, u32[]{:S(2)}, u32[]{:S(2)}) collective-permute-start(bf16[2,2,32,2176]{3,2,1,0:T(8,128)(2,1)S(1)} %pad_maximum_fusion.5), channel_id=1, source_target_pairs={{0,2},{1,3},{2,0},{3,1},{4,6},{5,7},{6,4},{7,5},{8,10},{9,11},{10,... | collective-permute-start | bytes 1671176 | tf_op jit(solution)/shard_map/ppermute | solution.py:112
  165.5 12.4 %collective-permute-start.10 = (bf16[2,2,32,2176]{3,2,1,0:T(8,128)(2,1)S(1)}, bf16[2,2,32,2176]{3,2,1,0:T(8,128)(2,1)S(1)}, u32[]{:S(2)}, u32[]{:S(2)}) collective-permute-start(bf16[2,2,32,2176]{3,2,1,0:T(8,128)(2,1)S(1)} %pad_maximum_fusion.4), channel_id=1, source_target_pairs={{0,4},{4,0},{8,12},{12,8},{16,20},{20,16},{24,28},{28,24},{1,5},{5... | collective-permute-start | bytes 1671176 | tf_op jit(solution)/shard_map/ppermute | solution.py:107
  167.1 12.1 %collective-permute-start.8 = (bf16[2,2,32,2176]{3,2,1,0:T(8,128)(2,1)S(1)}, bf16[2,2,32,2176]{3,2,1,0:T(8,128)(2,1)S(1)}, u32[]{:S(2)}, u32[]{:S(2)}) collective-permute-start(bf16[2,2,32,2176]{3,2,1,0:T(8,128)(2,1)S(1)} %pad_maximum_fusion.3), channel_id=1, source_target_pairs={{0,2},{1,3},{2,0},{3,1},{4,6},{5,7},{6,4},{7,5},{8,10},{9,11},{10,... | collective-permute-start | bytes 1671176 | tf_op jit(solution)/shard_map/ppermute | solution.py:112
  168.6 16.6 %slice-start = ((s8[6291456]{0:T(1024)(128)(4,1)}), s8[4194304]{0:T(1024)(128)(4,1)S(1)}, s32[]{:S(2)}) async-start(s8[6291456]{0:T(1024)(128)(4,1)} %bitcast.174), calls=%async_computation | async-start | bytes 8388608
  168.7 25.3 %collective-permute-start.24 = (bf16[512,2176]{1,0:T(8,128)(2,1)S(1)}, bf16[512,2176]{1,0:T(8,128)(2,1)S(1)}, u32[]{:S(2)}, u32[]{:S(2)}) collective-permute-start(bf16[512,2176]{1,0:T(8,128)(2,1)S(1)} %pad_maximum_fusion.2.tok_ref), channel_id=1, source_target_pairs={{0,1},{1,0},{2,3},{3,2},{4,5},{5,4},{6,7},{7,6},{8,9},{9,8},{10,11... | collective-permute-start | bytes 6684680 | tf_op jit(solution)/shard_map/ppermute | solution.py:117
  168.8 16.3 %slice-start.1 = ((s8[6291456]{0:T(1024)(128)(4,1)}), s8[2097152]{0:T(1024)(128)(4,1)S(1)}, s32[]{:S(2)}) async-start(s8[6291456]{0:T(1024)(128)(4,1)} %bitcast.174), calls=%async_computation.1 | async-start | bytes 4194304
  179.3 79.7 %collective-permute-start.11 = (bf16[512,2176]{1,0:T(8,128)(2,1)S(1)}, bf16[512,2176]{1,0:T(8,128)(2,1)S(1)}, u32[]{:S(2)}, u32[]{:S(2)}) collective-permute-start(bf16[512,2176]{1,0:T(8,128)(2,1)S(1)} %pad_maximum_fusion.1.tok_ref), channel_id=1, source_target_pairs={{0,1},{1,0},{2,3},{3,2},{4,5},{5,4},{6,7},{7,6},{8,9},{9,8},{10,11... | collective-permute-start | bytes 6684680 | tf_op jit(solution)/shard_map/ppermute | solution.py:117
  180.8 71.8 %collective-permute-start.35 = (bf16[1536,256]{1,0:T(8,128)(2,1)S(1)}, bf16[1536,256]{1,0:T(8,128)(2,1)S(1)}, u32[]{:S(2)}, u32[]{:S(2)}) collective-permute-start(bf16[1536,256]{1,0:T(8,128)(2,1)S(1)} %get-tuple-element.32), channel_id=1, source_target_pairs={{0,16},{4,20},{8,24},{12,28},{16,0},{20,4},{24,8},{28,12},{1,17},{... | collective-permute-start | bytes 2359304 | tf_op jit(solution)/shard_map/ppermute | solution.py:98
  180.8 82.2 %collective-permute-start.36 = (bf16[1536,256]{1,0:T(8,128)(2,1)}, bf16[1536,256]{1,0:T(8,128)(2,1)}, u32[]{:S(2)}, u32[]{:S(2)}) collective-permute-start(bf16[1536,256]{1,0:T(8,128)(2,1)} %get-tuple-element.31), channel_id=1, source_target_pairs={{0,4},{4,0},{8,12},{12,8},{16,20},{20,16},{24,28},{28,24},{1,5},{5... | collective-permute-start | bytes 2359304 | tf_op jit(solution)/shard_map/ppermute | solution.py:98
  181.3 88.2 %collective-permute-start.37 = (bf16[1536,256]{1,0:T(8,128)(2,1)}, bf16[1536,256]{1,0:T(8,128)(2,1)}, u32[]{:S(2)}, u32[]{:S(2)}) collective-permute-start(bf16[1536,256]{1,0:T(8,128)(2,1)} %get-tuple-element.30), channel_id=1, source_target_pairs={{0,20},{4,16},{8,28},{12,24},{16,4},{20,0},{24,12},{28,8},{1,21},{... | collective-permute-start | bytes 2359304 | tf_op jit(solution)/shard_map/ppermute | solution.py:98
  194.1 76.9 %collective-permute-start.39 = (bf16[1536,256]{1,0:T(8,128)(2,1)S(1)}, bf16[1536,256]{1,0:T(8,128)(2,1)S(1)}, u32[]{:S(2)}, u32[]{:S(2)}) collective-permute-start(bf16[1536,256]{1,0:T(8,128)(2,1)S(1)} %dynamic-slice_bitcast_fusion.6), channel_id=1, source_target_pairs={{0,24},{4,28},{8,16},{12,20},{16,8},{20,12},{24,0},{28,4},{1,25},{... | collective-permute-start | bytes 2359304 | tf_op jit(solution)/shard_map/ppermute | solution.py:98
  253.4 32.7 %collective-permute-start.25 = (bf16[512,2048]{1,0:T(8,128)(2,1)S(1)}, bf16[512,2048]{1,0:T(8,128)(2,1)}, u32[]{:S(2)}, u32[]{:S(2)}) collective-permute-start(bf16[512,2048]{1,0:T(8,128)(2,1)S(1)} %shard_map.179), channel_id=1, source_target_pairs={{0,1},{1,0},{2,3},{3,2},{4,5},{5,4},{6,7},{7,6},{8,9},{9,8},{10,11... | collective-permute-start | bytes 6291464 | tf_op jit(solution)/shard_map/ppermute | solution.py:117
  259.1 26.8 %collective-permute-start.38 = (bf16[1536,256]{1,0:T(8,128)(2,1)}, bf16[1536,256]{1,0:T(8,128)(2,1)S(1)}, u32[]{:S(2)}, u32[]{:S(2)}) collective-permute-start(bf16[1536,256]{1,0:T(8,128)(2,1)} %get-tuple-element.29), channel_id=1, source_target_pairs={{0,8},{4,12},{8,0},{12,4},{16,24},{20,28},{24,16},{28,20},{1,9},{5... | collective-permute-start | bytes 2359304 | tf_op jit(solution)/shard_map/ppermute | solution.py:98
  263.0 27.9 %collective-permute-start.12 = (bf16[512,2048]{1,0:T(8,128)(2,1)S(1)}, bf16[512,2048]{1,0:T(8,128)(2,1)S(1)}, u32[]{:S(2)}, u32[]{:S(2)}) collective-permute-start(bf16[512,2048]{1,0:T(8,128)(2,1)S(1)} %shard_map.177), channel_id=1, source_target_pairs={{0,1},{1,0},{2,3},{3,2},{4,5},{5,4},{6,7},{7,6},{8,9},{9,8},{10,11... | collective-permute-start | bytes 6291464 | tf_op jit(solution)/shard_map/ppermute | solution.py:117
  270.9 86.4 %collective-permute-start.40 = (bf16[1536,256]{1,0:T(8,128)(2,1)S(1)}, bf16[1536,256]{1,0:T(8,128)(2,1)S(1)}, u32[]{:S(2)}, u32[]{:S(2)}) collective-permute-start(bf16[1536,256]{1,0:T(8,128)(2,1)S(1)} %copy-done.11), channel_id=1, source_target_pairs={{0,12},{4,8},{8,4},{12,0},{16,28},{20,24},{24,20},{28,16},{1,13},{... | collective-permute-start | bytes 2359304 | tf_op jit(solution)/shard_map/ppermute | solution.py:98
  271.0 86.3 %collective-permute-start.41 = (bf16[1536,256]{1,0:T(8,128)(2,1)S(1)}, bf16[1536,256]{1,0:T(8,128)(2,1)S(1)}, u32[]{:S(2)}, u32[]{:S(2)}) collective-permute-start(bf16[1536,256]{1,0:T(8,128)(2,1)S(1)} %copy-done.10), channel_id=1, source_target_pairs={{0,28},{4,24},{8,20},{12,16},{16,12},{20,8},{24,4},{28,0},{1,29},{... | collective-permute-start | bytes 2359304 | tf_op jit(solution)/shard_map/ppermute | solution.py:98
  288.8 13.9 %collective-permute-start.26 = (bf16[2,2,32,2048]{3,2,1,0:T(8,128)(2,1)S(1)}, bf16[2,2,32,2048]{3,2,1,0:T(8,128)(2,1)S(1)}, u32[]{:S(2)}, u32[]{:S(2)}) collective-permute-start(bf16[2,2,32,2048]{3,2,1,0:T(8,128)(2,1)S(1)} %bitcast.201), channel_id=1, source_target_pairs={{0,2},{1,3},{2,0},{3,1},{4,6},{5,7},{6,4},{7,5},{8,10},{9,11},{10,... | collective-permute-start | bytes 1572872 | tf_op jit(solution)/shard_map/ppermute | solution.py:112
  290.4 40.5 %collective-permute-start.28 = (bf16[2,2,32,2048]{3,2,1,0:T(8,128)(2,1)S(1)}, bf16[2,2,32,2048]{3,2,1,0:T(8,128)(2,1)S(1)}, u32[]{:S(2)}, u32[]{:S(2)}) collective-permute-start(bf16[2,2,32,2048]{3,2,1,0:T(8,128)(2,1)S(1)} %bitcast.199), channel_id=1, source_target_pairs={{0,4},{4,0},{8,12},{12,8},{16,20},{20,16},{24,28},{28,24},{1,5},{5... | collective-permute-start | bytes 1572872 | tf_op jit(solution)/shard_map/ppermute | solution.py:107
  291.9 50.2 %collective-permute-start.15 = (bf16[2,2,32,2048]{3,2,1,0:T(8,128)(2,1)S(1)}, bf16[2,2,32,2048]{3,2,1,0:T(8,128)(2,1)S(1)}, u32[]{:S(2)}, u32[]{:S(2)}) collective-permute-start(bf16[2,2,32,2048]{3,2,1,0:T(8,128)(2,1)S(1)} %bitcast.200), channel_id=1, source_target_pairs={{0,4},{4,0},{8,12},{12,8},{16,20},{20,16},{24,28},{28,24},{1,5},{5... | collective-permute-start | bytes 1572872 | tf_op jit(solution)/shard_map/ppermute | solution.py:107
  302.8 41.0 %collective-permute-start.13 = (bf16[2,2,32,2048]{3,2,1,0:T(8,128)(2,1)S(1)}, bf16[2,2,32,2048]{3,2,1,0:T(8,128)(2,1)S(1)}, u32[]{:S(2)}, u32[]{:S(2)}) collective-permute-start(bf16[2,2,32,2048]{3,2,1,0:T(8,128)(2,1)S(1)} %bitcast.198), channel_id=1, source_target_pairs={{0,2},{1,3},{2,0},{3,1},{4,6},{5,7},{6,4},{7,5},{8,10},{9,11},{10,... | collective-permute-start | bytes 1572872 | tf_op jit(solution)/shard_map/ppermute | solution.py:112
  330.9 16.8 %collective-permute-start.27 = (bf16[2,32,2048]{2,1,0:T(8,128)(2,1)S(1)}, bf16[2,32,2048]{2,1,0:T(8,128)(2,1)S(1)}, u32[]{:S(2)}, u32[]{:S(2)}) collective-permute-start(bf16[2,32,2048]{2,1,0:T(8,128)(2,1)S(1)} %slice_bitcast_fusion.2), channel_id=1, source_target_pairs={{0,4},{4,0},{8,12},{12,8},{16,20},{20,16},{24,28},{28,24},{1,5},{5... | collective-permute-start | bytes 786440 | tf_op jit(solution)/shard_map/ppermute | solution.py:107
  342.1 9.2 %collective-permute-start.29 = (bf16[2,32,2048]{2,1,0:T(8,128)(2,1)S(1)}, bf16[2,32,2048]{2,1,0:T(8,128)(2,1)S(1)}, u32[]{:S(2)}, u32[]{:S(2)}) collective-permute-start(bf16[2,32,2048]{2,1,0:T(8,128)(2,1)S(1)} %slice_bitcast_fusion), channel_id=1, source_target_pairs={{0,2},{1,3},{2,0},{3,1},{4,6},{5,7},{6,4},{7,5},{8,10},{9,11},{10,... | collective-permute-start | bytes 786440 | tf_op jit(solution)/shard_map/ppermute | solution.py:112
  343.7 12.1 %collective-permute-start.16 = (bf16[2,32,2048]{2,1,0:T(8,128)(2,1)S(1)}, bf16[2,32,2048]{2,1,0:T(8,128)(2,1)S(1)}, u32[]{:S(2)}, u32[]{:S(2)}) collective-permute-start(bf16[2,32,2048]{2,1,0:T(8,128)(2,1)S(1)} %slice_bitcast_fusion.4), channel_id=1, source_target_pairs={{0,2},{1,3},{2,0},{3,1},{4,6},{5,7},{6,4},{7,5},{8,10},{9,11},{10,... | collective-permute-start | bytes 786440 | tf_op jit(solution)/shard_map/ppermute | solution.py:112
  347.6 8.3 %collective-permute-start.14 = (bf16[2,32,2048]{2,1,0:T(8,128)(2,1)S(1)}, bf16[2,32,2048]{2,1,0:T(8,128)(2,1)S(1)}, u32[]{:S(2)}, u32[]{:S(2)}) collective-permute-start(bf16[2,32,2048]{2,1,0:T(8,128)(2,1)S(1)} %slice_bitcast_fusion.6), channel_id=1, source_target_pairs={{0,4},{4,0},{8,12},{12,8},{16,20},{20,16},{24,28},{28,24},{1,5},{5... | collective-permute-start | bytes 786440 | tf_op jit(solution)/shard_map/ppermute | solution.py:107
  351.4 11.0 %collective-permute-start.31 = (bf16[64,2048]{1,0:T(8,128)(2,1)S(1)}, bf16[64,2048]{1,0:T(8,128)(2,1)S(1)}, u32[]{:S(2)}, u32[]{:S(2)}) collective-permute-start(bf16[64,2048]{1,0:T(8,128)(2,1)S(1)} %get-tuple-element.53), channel_id=1, source_target_pairs={{0,8},{4,12},{8,16},{12,20},{16,24},{20,28},{24,0},{28,4},{1,9},{5... | collective-permute-start | bytes 786440 | tf_op jit(solution)/shard_map/ppermute | solution.py:93
  355.8 15.1 %collective-permute-start.30 = (bf16[64,2048]{1,0:T(8,128)(2,1)S(1)}, bf16[64,2048]{1,0:T(8,128)(2,1)S(1)}, u32[]{:S(2)}, u32[]{:S(2)}) collective-permute-start(bf16[64,2048]{1,0:T(8,128)(2,1)S(1)} %get-tuple-element.52), channel_id=1, source_target_pairs={{0,16},{4,20},{8,24},{12,28},{16,0},{20,4},{24,8},{28,12},{1,17},{... | collective-permute-start | bytes 786440 | tf_op jit(solution)/shard_map/ppermute | solution.py:93
  356.0 16.1 %copy-start.1 = (bf16[512,2048]{1,0:T(8,128)(2,1)S(1)}, bf16[512,2048]{1,0:T(8,128)(2,1)}, u32[]{:S(2)}) copy-start(bf16[512,2048]{1,0:T(8,128)(2,1)} %param.27) | copy-start | bytes 6291460
  356.0 15.2 %collective-permute-start.17 = (bf16[64,2048]{1,0:T(8,128)(2,1)S(1)}, bf16[64,2048]{1,0:T(8,128)(2,1)S(1)}, u32[]{:S(2)}, u32[]{:S(2)}) collective-permute-start(bf16[64,2048]{1,0:T(8,128)(2,1)S(1)} %fusion.37), channel_id=1, source_target_pairs={{0,24},{4,28},{8,0},{12,4},{16,8},{20,12},{24,16},{28,20},{1,25},{... | collective-permute-start | bytes 786440 | tf_op jit(solution)/shard_map/ppermute | solution.py:93
  (18 other events, 125.8 us)
where the time goes:
time: 376 us; the launch traced here: 372 us
  waiting for transfers between devices  225 us (60%)
  starting transfers between devices  47.6 us (13%)
  between operations  29.8 us (8%)
  other arithmetic  25.4 us (7%)
  local copies, waits for them, and re-layouts  23.3 us (6%)
  Pallas kernels  15.3 us (4%)
  matrix products  5.67 us (2%)
    ppermute x10, waiting for transfers between devices, swap(): return lax.ppermute(value, 'req', [(i, i ^ mask) for i in range(count)])  72.2 us
    ppermute x9, waiting for transfers between devices, flip_pair(): return lax.ppermute(value, 'req', [(i, i ^ 1) for i in range(count)])  68.4 us
    ppermute x9, waiting for transfers between devices, turn_pairs(): lax.ppermute(value, 'req', [(i, (i + 2 * step) % count) for i in range(co...  67.4 us
    ppermute x9, waiting for transfers between devices, flip_chip(): return lax.ppermute(value, 'exp', [(i, i ^ 2) for i in range(count)])  17 us
    pallas_call x4, Pallas kernels, run_experts(): pl.pallas_call(experts_kernel, out_shape=jax.ShapeDtypeStruct((count, wid...  15.3 us
    ppermute x9, starting transfers between devices, flip_chip(): return lax.ppermute(value, 'exp', [(i, i ^ 2) for i in range(count)])  12.7 us
    ppermute x10, starting transfers between devices, swap(): return lax.ppermute(value, 'req', [(i, i ^ mask) for i in range(count)])  12.4 us
    squeeze x5, local copies, waits for them, and re-layouts, pick(): return lax.dynamic_index_in_dim(value, index, axis, keepdims=False)  12 us
  transfers between devices with their start and end apart: 42, of which 21 were waited for; matrix products, arithmetic and copies ran while one was open for 11% of the time, Pallas kernels for 4%

commit v1 on v0

--- a/solution.py
+++ b/solution.py
@@ -216,30 +216,58 @@
     return jnp.concatenate(held)
 
 
+def copy_kernel(index_ref, source_ref, out_ref):
+    out_ref[...] = source_ref[...]
+
+
+def take_chunks(source, index, part, parts):
+    _, rows, width = source.shape
+    size = rows // parts
+    return pl.pallas_call(
+        copy_kernel,
+        out_shape=jax.ShapeDtypeStruct((index.shape[0], size, width), source.dtype),
+        grid_spec=pltpu.PrefetchScalarGridSpec(
+            num_scalar_prefetch=1,
+            grid=(index.shape[0],),
+            in_specs=[pl.BlockSpec((1, size, width), lambda i, index: (index[i], part, 0))],
+            out_specs=pl.BlockSpec((1, size, width), lambda i, index: (i, 0, 0)),
+        ),
+        cost_estimate=pl.CostEstimate(
+            flops=0, bytes_accessed=4 * index.shape[0] * size * width, transcendentals=0
+        ),
+    )(index, source)
+
+
 def collect_replicas(held, source_slot, slots_here, events):
     me = lax.axis_index("req")
     count = lax.axis_size("req")
     half = count // 2
-    spot = me % half
-    arrived = {}
-    order = [half + mask for mask in range(half)] + list(range(half))
-    for place, mask in enumerate(order):
-        source = held
-        if place < 2 or mask == 1:
-            source = after(held, *events["spread"])
-        elif place == 2:
-            source = after(held, *events["gathered"])
-        elif mask:
-            source = after(held, *events["mixed"])
-        slot = pick(source_slot, me ^ mask, 0)
-        index = (spot ^ (slot // slots_here % half)) * slots_here + slot % slots_here
-        piece = pick(source, index, 0)
-        arrived[mask] = swap(piece, mask) if mask else piece
-    same = pick(source_slot, me, 0) // slots_here // half == me // half
-    result = jnp.zeros((half,) + held.shape[1:], held.dtype)
-    for mask in range(half):
-        piece = jnp.where(same, arrived[mask], arrived[half + mask])
-        result = lax.dynamic_update_index_in_dim(result, piece, spot ^ mask, 0)
+    pair_count = count // 2
+    side = me % 2
+    columns = [[2 * i + k for i in range(pair_count)] for k in range(2)]
+    spots = source_slot // slots_here % half
+    index = ((me % half) ^ spots) * slots_here + source_slot % slots_here
+    halves = source_slot // slots_here // half
+    parts = 2
+    size, width = held.shape[1] // parts, held.shape[2]
+    result = jnp.zeros((half // 2, 2, parts, size, width), held.dtype)
+    for part in range(parts):
+        source = after(held, *events["spread" if part == 0 else "mixed"])
+        outgoing = take_chunks(source, index, part, parts)
+        outgoing = outgoing.reshape(pair_count, 2, size, width)
+        arrived = lax.all_to_all(
+            outgoing, "req", 0, 0, axis_index_groups=columns, tiled=True
+        )
+
+        def wanted_by(receiver):
+            begin = pick(halves, receiver, 0) * (half // 2)
+            where = (begin, receiver % 2, 0, 0)
+            return lax.dynamic_slice(arrived, where, (half // 2, 1, size, width))
+
+        swapped = swap(wanted_by(me ^ 1), 1)
+        for rows, column in ((wanted_by(me), side), (swapped, 1 - side)):
+            where = (0, column, part, 0, 0)
+            result = lax.dynamic_update_slice(result, rows[:, :, None], where)
     return result
 
 

time: 376 us -> 378 us (level)
  waiting for transfers between devices: 225 us -> 201 us
  Pallas kernels: 15.3 us -> 35.9 us
  between operations: 29.8 us -> 10.5 us
  local copies, waits for them, and re-layouts: 23.3 us -> 33.9 us
  other arithmetic: 25.4 us -> 35.3 us
  starting transfers between devices: 47.6 us -> 54.5 us
    ppermute x10 -> x5, waiting for transfers between devices: 72.2 us -> 4.52 us  [swap(): return lax.ppermute(value, 'req', [(i, i ^ mask) for i in range(count)])]
    all_to_all x0 -> x2, waiting for transfers between devices: none -> 67 us  [collect_replicas(): lax.all_to_all(outgoing, 'req', 0, 0, axis_index_groups=columns, tiled=True)]
    ppermute x9, waiting for transfers between devices: 67.4 us -> 42.4 us  [turn_pairs(): lax.ppermute(value, 'req', [(i, (i + 2 * step) % count) for i in range(co...]
    pallas_call x0 -> x2, Pallas kernels: none -> 13.6 us  [take_chunks(): pl.pallas_call(copy_kernel, out_shape=jax.ShapeDtypeStruct((index.shape[0...]
    ppermute x9, waiting for transfers between devices: 17 us -> 29.5 us  [flip_chip(): return lax.ppermute(value, 'exp', [(i, i ^ 2) for i in range(count)])]
    ppermute x9, waiting for transfers between devices: 68.4 us -> 57.6 us  [flip_pair(): return lax.ppermute(value, 'req', [(i, i ^ 1) for i in range(count)])]
    all_to_all x0 -> x2, starting transfers between devices: none -> 9.49 us  [collect_replicas(): lax.all_to_all(outgoing, 'req', 0, 0, axis_index_groups=columns, tiled=True)]
    ppermute x9, starting transfers between devices: 9.86 us -> 18.9 us  [turn_pairs(): lax.ppermute(value, 'req', [(i, (i + 2 * step) % count) for i in range(co...]
  transfers between devices with their start and end apart: 42 -> 39, of which waited for: 21 -> 15; matrix products, arithmetic and copies ran while one was open for 11% -> 15% of each run, Pallas kernels for 4% -> 10%
where the time goes in v1:
time: 378 us; the launch traced here: 377 us
  waiting for transfers between devices  201 us (53%)
  starting transfers between devices  54.5 us (14%)
  Pallas kernels  35.9 us (9%)
  other arithmetic  35.3 us (9%)
  local copies, waits for them, and re-layouts  33.9 us (9%)
  between operations  10.5 us (3%)
  matrix products  5.67 us (2%)
    all_to_all x2, waiting for transfers between devices, collect_replicas(): lax.all_to_all(outgoing, 'req', 0, 0, axis_index_groups=columns, tiled=True)  67 us
    ppermute x9, waiting for transfers between devices, flip_pair(): return lax.ppermute(value, 'req', [(i, i ^ 1) for i in range(count)])  57.6 us
    ppermute x9, waiting for transfers between devices, turn_pairs(): lax.ppermute(value, 'req', [(i, (i + 2 * step) % count) for i in range(co...  42.4 us
    ppermute x9, waiting for transfers between devices, flip_chip(): return lax.ppermute(value, 'exp', [(i, i ^ 2) for i in range(count)])  29.5 us
    pallas_call x4, Pallas kernels, run_experts(): pl.pallas_call(experts_kernel, out_shape=jax.ShapeDtypeStruct((count, wid...  22.3 us
    ppermute x9, starting transfers between devices, turn_pairs(): lax.ppermute(value, 'req', [(i, (i + 2 * step) % count) for i in range(co...  18.9 us
    pallas_call x2, Pallas kernels, take_chunks(): pl.pallas_call(copy_kernel, out_shape=jax.ShapeDtypeStruct((index.shape[0...  13.6 us
    unnamed x51, local copies, waits for them, and re-layouts  10.8 us
  transfers between devices with their start and end apart: 39, of which 15 were waited for; matrix products, arithmetic and copies ran while one was open for 15% of the time, Pallas kernels for 10%

profile of v1, /device:TPU:0, one launch (start us, length us, event | category | flops | bytes accessed | tf_op | source)
XLA Modules:
  0.0 376.7 jit_solution(17685209601878593977)
XLA Ops:
  0.7 1.7 fusion.72
  2.4 3.0 collective-permute-start
  5.4 2.6 collective-permute-start.1
  31.2 1.6 collective-permute-start.3
  32.9 3.3 collective-permute-done.3
  36.4 3.3 fusion.81
  39.7 1.7 fusion.6
  43.9 4.8 %dynamic-slice_bitcast_fusion.3 = (bf16[2,1536,256]{2,1,0:T(8,128)(2,1)}, bf16[2,1536,256]{2,1,0:T(8,128)(2,1)}, bf16[2,1536,256]{2,1,0:T(8,128)(2,1)}) fusion(bf16[2,4,1536,256]{3,2,1,0:T(8,128)(2,1)} %bitcast.160, s32[]{:T(128)S(6)} %select_n.259, s32[]{:T(128)S(6)} %select_n.260, s32[]{:T(128)S(6)} %select_n.261), kind=kLoop, calls=%fused_computation.12 | loop fusion | bytes 9437196 | tf_op jit(solution)/shard_map/jit(dynamic_index_in_dim)/squeeze | solution.py:121
  48.7 1.6 collective-permute-start.32
  54.0 6.3 %collective-permute-done.5 = bf16[64,2048]{1,0:T(8,128)(2,1)S(1)} collective-permute-done((bf16[64,2048]{1,0:T(8,128)(2,1)S(1)}, bf16[64,2048]{1,0:T(8,128)(2,1)S(1)}, u32[]{:S(2)}, u32[]{:S(2)}) %collective-permute-start.5) | collective-permute-done | bytes 262176 | tf_op jit(solution)/shard_map/ppermute | solution.py:112
  65.1 2.2 collective-permute-start.19
  67.3 26.2 %collective-permute-done.6 = bf16[64,2176]{1,0:T(8,128)(2,1)S(1)} collective-permute-done((bf16[64,2176]{1,0:T(8,128)(2,1)S(1)}, bf16[64,2176]{1,0:T(8,128)(2,1)S(1)}, u32[]{:S(2)}, u32[]{:S(2)}) %collective-permute-start.6) | collective-permute-done | bytes 278560 | tf_op jit(solution)/shard_map/ppermute | solution.py:93
  93.9 4.0 %collective-permute-done.18 = bf16[64,2176]{1,0:T(8,128)(2,1)S(1)} collective-permute-done((bf16[64,2176]{1,0:T(8,128)(2,1)S(1)}, bf16[64,2176]{1,0:T(8,128)(2,1)S(1)}, u32[]{:S(2)}, u32[]{:S(2)}) %collective-permute-start.18) | collective-permute-done | bytes 278560 | tf_op jit(solution)/shard_map/ppermute | solution.py:93
  97.9 7.0 %collective-permute-done.19 = bf16[64,2176]{1,0:T(8,128)(2,1)S(1)} collective-permute-done((bf16[64,2176]{1,0:T(8,128)(2,1)S(1)}, bf16[64,2176]{1,0:T(8,128)(2,1)S(1)}, u32[]{:S(2)}, u32[]{:S(2)}) %collective-permute-start.19) | collective-permute-done | bytes 278560 | tf_op jit(solution)/shard_map/ppermute | solution.py:93
  107.6 11.5 %collective-permute-done.9 = bf16[2,32,2176]{2,1,0:T(8,128)(2,1)S(1)} collective-permute-done((bf16[2,32,2176]{2,1,0:T(8,128)(2,1)S(1)}, bf16[2,32,2176]{2,1,0:T(8,128)(2,1)S(1)}, u32[]{:S(2)}, u32[]{:S(2)}) %collective-permute-start.9) | collective-permute-done | bytes 278560 | tf_op jit(solution)/shard_map/ppermute | solution.py:112
  120.7 1.6 collective-permute-start.10
  123.0 11.7 %collective-permute-done.8 = bf16[2,2,32,2176]{3,2,1,0:T(8,128)(2,1)S(1)} collective-permute-done((bf16[2,2,32,2176]{3,2,1,0:T(8,128)(2,1)S(1)}, bf16[2,2,32,2176]{3,2,1,0:T(8,128)(2,1)S(1)}, u32[]{:S(2)}, u32[]{:S(2)}) %collective-permute-start.8) | collective-permute-done | bytes 557088 | tf_op jit(solution)/shard_map/ppermute | solution.py:112
  135.2 32.1 %collective-permute-done.10 = bf16[2,2,32,2176]{3,2,1,0:T(8,128)(2,1)S(1)} collective-permute-done((bf16[2,2,32,2176]{3,2,1,0:T(8,128)(2,1)S(1)}, bf16[2,2,32,2176]{3,2,1,0:T(8,128)(2,1)S(1)}, u32[]{:S(2)}, u32[]{:S(2)}) %collective-permute-start.10) | collective-permute-done | bytes 557088 | tf_op jit(solution)/shard_map/ppermute | solution.py:107
  170.6 8.1 %collective-permute-done.23 = bf16[2,2,32,2176]{3,2,1,0:T(8,128)(2,1)S(1)} collective-permute-done((bf16[2,2,32,2176]{3,2,1,0:T(8,128)(2,1)S(1)}, bf16[2,2,32,2176]{3,2,1,0:T(8,128)(2,1)S(1)}, u32[]{:S(2)}, u32[]{:S(2)}) %collective-permute-start.23) | collective-permute-done | bytes 557088 | tf_op jit(solution)/shard_map/ppermute | solution.py:107
  178.8 1.6 pad_maximum_fusion.2.tok_ref
  181.0 5.1 %pad_maximum_fusion.source_ref = bf16[8,1536,256]{2,1,0:T(8,128)(2,1)} fusion(bf16[2,1536,256]{2,1,0:T(8,128)(2,1)S(1)} %collective-permute-done.34, bf16[2,1536,256]{2,1,0:T(8,128)(2,1)} %collective-permute-done.33, bf16[2,1536,256]{2,1,0:T(8,128)(2,1)} %collective-permute-done.32, bf16[2,1536,256]{2,1,0:T(8,128)(2,1)S(1)} %copy-done.8), kind=kLoop, calls=%fused_computation.1 | loop fusion | flops 9437184 | bytes 12582912 | tf_op jit(solution)/shard_map/concatenate | solution.py:216
  186.1 6.8 %shard_map.180 = bf16[8,768,256]{2,1,0:T(8,128)(2,1)} custom-call(s32[8]{0:T(128)} %fusion.53.index_ref, bf16[8,1536,256]{2,1,0:T(8,128)(2,1)} %pad_maximum_fusion.source_ref), custom_call_target="tpu_custom_call" | custom-call | bytes 6291456 | tf_op jit(solution)/shard_map/pallas_call | solution.py:226
  192.9 4.8 %all-to-all-start = ((bf16[4,2,768,256]{3,2,1,0:T(8,128)(2,1)}), bf16[4,2,768,256]{3,2,1,0:T(8,128)(2,1)}, u32[]{:S(2)}, u32[]{:S(2)}) async-start(bf16[4,2,768,256]{3,2,1,0:T(8,128)(2,1)} %bitcast.163), calls=%async_computation | async-start | bytes 6291456 | tf_op jit(solution)/shard_map/all_to_all | solution.py:258
  197.7 2.8 copy-done.2
  200.5 6.0 %shard_map.177 = bf16[512,2048]{1,0:T(8,128)(2,1)} custom-call(s32[1]{0:T(128)} %bitcast.32.first_slot_ref, bf16[512,2176]{1,0:T(8,128)(2,1)} %collective-permute-done.11.tok_ref, bf16[2,3,2048,256]{3,2,1,0:T(8,128)(2,1)S(1)} %copy-done.2), custom_call_target="tpu_custom_call" | custom-call | flops 3221225472 | bytes 10485760 | tf_op jit(solution)/shard_map/pallas_call | solution.py:72
  207.1 6.1 %shard_map.179 = bf16[512,2048]{1,0:T(8,128)(2,1)} custom-call(s32[1]{0:T(128)} %bitcast.32.first_slot_ref, bf16[512,2176]{1,0:T(8,128)(2,1)} %collective-permute-done.24.tok_ref, bf16[2,3,2048,256]{3,2,1,0:T(8,128)(2,1)S(1)} %copy-done.2), custom_call_target="tpu_custom_call" | custom-call | flops 3221225472 | bytes 10485760 | tf_op jit(solution)/shard_map/pallas_call | solution.py:72
  215.2 2.8 copy-done.3
  218.0 5.1 %shard_map.178 = bf16[512,2048]{1,0:T(8,128)(2,1)S(1)} custom-call(s32[1]{0:T(128)} %bitcast.32.first_slot_ref, bf16[512,2176]{1,0:T(8,128)(2,1)} %pad_maximum_fusion.2.tok_ref, bf16[2,3,2048,256]{3,2,1,0:T(8,128)(2,1)S(1)} %copy-done.3), custom_call_target="tpu_custom_call" | custom-call | flops 3221225472 | bytes 10485760 | tf_op jit(solution)/shard_map/pallas_call | solution.py:72
  224.4 5.1 %shard_map.176 = bf16[512,2048]{1,0:T(8,128)(2,1)S(1)} custom-call(s32[1]{0:T(128)} %bitcast.32.first_slot_ref, bf16[512,2176]{1,0:T(8,128)(2,1)} %pad_maximum_fusion.1.tok_ref, bf16[2,3,2048,256]{3,2,1,0:T(8,128)(2,1)S(1)} %copy-done.3), custom_call_target="tpu_custom_call" | custom-call | flops 3221225472 | bytes 10485760 | tf_op jit(solution)/shard_map/pallas_call | solution.py:72
  229.5 6.8 %shard_map.181 = bf16[8,768,256]{2,1,0:T(8,128)(2,1)} custom-call(s32[8]{0:T(128)} %fusion.53.index_ref, bf16[8,1536,256]{2,1,0:T(8,128)(2,1)} %pad_maximum_fusion.source_ref), custom_call_target="tpu_custom_call" | custom-call | bytes 6291456 | tf_op jit(solution)/shard_map/pallas_call | solution.py:226
  236.3 2.4 add_convert_fusion.1
  242.2 2.4 add_convert_fusion
  247.7 21.5 %all-to-all-done = bf16[4,2,768,256]{3,2,1,0:T(8,128)(2,1)} async-done(((bf16[4,2,768,256]{3,2,1,0:T(8,128)(2,1)}), bf16[4,2,768,256]{3,2,1,0:T(8,128)(2,1)}, u32[]{:S(2)}, u32[]{:S(2)}) %all-to-all-start) | async-done | bytes 3145760 | tf_op jit(solution)/shard_map/all_to_all | solution.py:258
  269.2 4.7 %all-to-all-start.1 = ((bf16[4,2,768,256]{3,2,1,0:T(8,128)(2,1)}), bf16[4,2,768,256]{3,2,1,0:T(8,128)(2,1)}, u32[]{:S(2)}, u32[]{:S(2)}) async-start(bf16[4,2,768,256]{3,2,1,0:T(8,128)(2,1)} %bitcast.162), calls=%async_computation.1 | async-start | bytes 6291456 | tf_op jit(solution)/shard_map/all_to_all | solution.py:258
  273.9 2.1 constant_dynamic-slice_fusion.1
  279.0 1.6 fusion.10
  284.2 1.6 collective-permute-start.29
  286.9 1.6 collective-permute-start.27
  288.5 13.7 %collective-permute-done.14 = bf16[2,32,2048]{2,1,0:T(8,128)(2,1)S(1)} collective-permute-done((bf16[2,32,2048]{2,1,0:T(8,128)(2,1)S(1)}, bf16[2,32,2048]{2,1,0:T(8,128)(2,1)S(1)}, u32[]{:S(2)}, u32[]{:S(2)}) %collective-permute-start.14) | collective-permute-done | bytes 262176 | tf_op jit(solution)/shard_map/ppermute | solution.py:107
  302.4 3.9 %collective-permute-start.17 = (bf16[64,2048]{1,0:T(8,128)(2,1)S(1)}, bf16[64,2048]{1,0:T(8,128)(2,1)}, u32[]{:S(2)}, u32[]{:S(2)}) collective-permute-start(bf16[64,2048]{1,0:T(8,128)(2,1)S(1)} %fusion.37), channel_id=1, source_target_pairs={{0,24},{4,28},{8,0},{12,4},{16,8},{20,12},{24,16},{28,20},{1,25},{... | collective-permute-start | bytes 786440 | tf_op jit(solution)/shard_map/ppermute | solution.py:93
  307.5 2.6 collective-permute-start.30
  311.6 45.5 %all-to-all-done.1 = bf16[4,2,768,256]{3,2,1,0:T(8,128)(2,1)} async-done(((bf16[4,2,768,256]{3,2,1,0:T(8,128)(2,1)}), bf16[4,2,768,256]{3,2,1,0:T(8,128)(2,1)}, u32[]{:S(2)}, u32[]{:S(2)}) %all-to-all-start.1) | async-done | bytes 3145760 | tf_op jit(solution)/shard_map/all_to_all | solution.py:258
  358.2 1.6 collective-permute-start.36
  359.8 2.2 bitcast_dynamic-update-slice_fusion.1
  362.0 5.2 %collective-permute-done.30 = bf16[64,2048]{1,0:T(8,128)(2,1)} collective-permute-done((bf16[64,2048]{1,0:T(8,128)(2,1)}, bf16[64,2048]{1,0:T(8,128)(2,1)}, u32[]{:S(2)}, u32[]{:S(2)}) %collective-permute-start.30) | collective-permute-done | bytes 262176 | tf_op jit(solution)/shard_map/ppermute | solution.py:93
  367.3 2.0 fusion.17
  369.2 2.1 bitcast_dynamic-update-slice_fusion.2
  371.3 4.5 %collective-permute-done.36 = bf16[2,1,768,256]{3,2,1,0:T(8,128)(2,1)S(1)} collective-permute-done((bf16[2,1,768,256]{3,2,1,0:T(8,128)(2,1)S(1)}, bf16[2,1,768,256]{3,2,1,0:T(8,128)(2,1)S(1)}, u32[]{:S(2)}, u32[]{:S(2)}) %collective-permute-start.36) | collective-permute-done | bytes 786464 | tf_op jit(solution)/shard_map/ppermute | solution.py:98
  (188 shorter events, 58.1 us)
Async XLA Ops:
  0.6 41.0 %copy-start = (bf16[512,2048]{1,0:T(8,128)(2,1)S(1)}, bf16[512,2048]{1,0:T(8,128)(2,1)}, u32[]{:S(2)}) copy-start(bf16[512,2048]{1,0:T(8,128)(2,1)} %param.27) | copy-start | bytes 6291460
  0.6 15.7 %copy-start.13 = (bf16[256,512]{1,0:T(8,128)(2,1)S(1)}, bf16[256,512]{1,0:T(8,128)(2,1)}, u32[]{:S(2)}) copy-start(bf16[256,512]{1,0:T(8,128)(2,1)} %param.19) | copy-start | bytes 786436
  2.4 27.6 %collective-permute-start = (bf16[2,2,32,512]{3,2,1,0:T(8,128)(2,1)}, bf16[2,2,32,512]{3,2,1,0:T(8,128)(2,1)}, u32[]{:S(2)}, u32[]{:S(2)}) collective-permute-start(bf16[2,2,32,512]{3,2,1,0:T(8,128)(2,1)} %get-tuple-element.57), channel_id=1, source_target_pairs={{0,8},{4,12},{8,16},{12,20},{16,24},{20,28},{24,0},{28,4},{1,9},{5... | collective-permute-start | bytes 393224 | tf_op jit(solution)/shard_map/ppermute | solution.py:93
  5.4 24.6 %collective-permute-start.1 = (bf16[2,2,32,512]{3,2,1,0:T(8,128)(2,1)}, bf16[2,2,32,512]{3,2,1,0:T(8,128)(2,1)}, u32[]{:S(2)}, u32[]{:S(2)}) collective-permute-start(bf16[2,2,32,512]{3,2,1,0:T(8,128)(2,1)} %get-tuple-element.57), channel_id=1, source_target_pairs={{0,16},{4,20},{8,24},{12,28},{16,0},{20,4},{24,8},{28,12},{1,17},{... | collective-permute-start | bytes 393224 | tf_op jit(solution)/shard_map/ppermute | solution.py:93
  8.0 22.0 %collective-permute-start.2 = (bf16[2,2,32,512]{3,2,1,0:T(8,128)(2,1)}, bf16[2,2,32,512]{3,2,1,0:T(8,128)(2,1)}, u32[]{:S(2)}, u32[]{:S(2)}) collective-permute-start(bf16[2,2,32,512]{3,2,1,0:T(8,128)(2,1)} %get-tuple-element.57), channel_id=1, source_target_pairs={{0,24},{4,28},{8,0},{12,4},{16,8},{20,12},{24,16},{28,20},{1,25},{... | collective-permute-start | bytes 393224 | tf_op jit(solution)/shard_map/ppermute | solution.py:93
  19.7 7.3 %copy-start.14 = (bf16[256,512]{1,0:T(8,128)(2,1)S(1)}, bf16[256,512]{1,0:T(8,128)(2,1)}, u32[]{:S(2)}) copy-start(bf16[256,512]{1,0:T(8,128)(2,1)} %param.20) | copy-start | bytes 786436
  31.2 5.0 %collective-permute-start.3 = (bf16[2,2,32,512]{3,2,1,0:T(8,128)(2,1)S(1)}, bf16[2,2,32,512]{3,2,1,0:T(8,128)(2,1)S(1)}, u32[]{:S(2)}, u32[]{:S(2)}) collective-permute-start(bf16[2,2,32,512]{3,2,1,0:T(8,128)(2,1)S(1)} %pad_maximum_fusion.13), channel_id=1, source_target_pairs={{0,4},{4,0},{8,12},{12,8},{16,20},{20,16},{24,28},{28,24},{1,5},{5... | collective-permute-start | bytes 393224 | tf_op jit(solution)/shard_map/ppermute | solution.py:107
  43.8 7.2 %collective-permute-start.4 = (bf16[2,64,2048]{2,1,0:T(8,128)(2,1)S(1)}, bf16[2,64,2048]{2,1,0:T(8,128)(2,1)S(1)}, u32[]{:S(2)}, u32[]{:S(2)}) collective-permute-start(bf16[2,64,2048]{2,1,0:T(8,128)(2,1)S(1)} %fusion.11), channel_id=1, source_target_pairs={{0,1},{1,0},{2,3},{3,2},{4,5},{5,4},{6,7},{7,6},{8,9},{9,8},{10,11... | collective-permute-start | bytes 1572872 | tf_op jit(solution)/shard_map/ppermute | solution.py:117
  43.9 7.1 %copy-start.7 = (f32[2,2,64,2048]{3,2,1,0:T(8,128)S(1)}, f32[2,2,64,2048]{3,2,1,0:T(8,128)}, u32[]{:S(2)}) copy-start(f32[2,2,64,2048]{3,2,1,0:T(8,128)} %copy-done.6) | copy-start | bytes 6291460
  48.7 5.0 %copy-start.20 = (s32[16]{0:T(128)S(1)}, s32[16]{0:T(128)}, u32[]{:S(2)}) copy-start(s32[16]{0:T(128)} %param.31) | copy-start | bytes 196
  48.7 11.6 %copy-start.15 = (bf16[64,2048]{1,0:T(8,128)(2,1)S(1)}, bf16[64,2048]{1,0:T(8,128)(2,1)}, u32[]{:S(2)}) copy-start(bf16[64,2048]{1,0:T(8,128)(2,1)} %param.17) | copy-start | bytes 786436
  48.7 132.3 %collective-permute-start.32 = (bf16[2,1536,256]{2,1,0:T(8,128)(2,1)}, bf16[2,1536,256]{2,1,0:T(8,128)(2,1)}, u32[]{:S(2)}, u32[]{:S(2)}) collective-permute-start(bf16[2,1536,256]{2,1,0:T(8,128)(2,1)} %get-tuple-element.28), channel_id=1, source_target_pairs={{0,4},{4,0},{8,12},{12,8},{16,20},{20,16},{24,28},{28,24},{1,5},{5... | collective-permute-start | bytes 4718600 | tf_op jit(solution)/shard_map/ppermute | solution.py:98
  50.3 130.7 %collective-permute-start.33 = (bf16[2,1536,256]{2,1,0:T(8,128)(2,1)}, bf16[2,1536,256]{2,1,0:T(8,128)(2,1)}, u32[]{:S(2)}, u32[]{:S(2)}) collective-permute-start(bf16[2,1536,256]{2,1,0:T(8,128)(2,1)} %get-tuple-element.29), channel_id=1, source_target_pairs={{0,8},{4,12},{8,0},{12,4},{16,24},{20,28},{24,16},{28,20},{1,9},{5... | collective-permute-start | bytes 4718600 | tf_op jit(solution)/shard_map/ppermute | solution.py:98
  51.0 10.6 %copy-start.16 = (f32[2048]{0:T(1024)S(1)}, f32[2048]{0:T(1024)}, u32[]{:S(2)}) copy-start(f32[2048]{0:T(1024)} %param.28) | copy-start | bytes 24580
  52.1 8.2 %collective-permute-start.5 = (bf16[64,2048]{1,0:T(8,128)(2,1)S(1)}, bf16[64,2048]{1,0:T(8,128)(2,1)S(1)}, u32[]{:S(2)}, u32[]{:S(2)}) collective-permute-start(bf16[64,2048]{1,0:T(8,128)(2,1)S(1)} %fusion.31), channel_id=1, source_target_pairs={{0,2},{1,3},{2,0},{3,1},{4,6},{5,7},{6,4},{7,5},{8,10},{9,11},{10,... | collective-permute-start | bytes 786440 | tf_op jit(solution)/shard_map/ppermute | solution.py:112
  61.8 31.8 %collective-permute-start.6 = (bf16[64,2176]{1,0:T(8,128)(2,1)S(1)}, bf16[64,2176]{1,0:T(8,128)(2,1)S(1)}, u32[]{:S(2)}, u32[]{:S(2)}) collective-permute-start(bf16[64,2176]{1,0:T(8,128)(2,1)S(1)} %concatenate.40), channel_id=1, source_target_pairs={{0,8},{4,12},{8,16},{12,20},{16,24},{20,28},{24,0},{28,4},{1,9},{5... | collective-permute-start | bytes 835592 | tf_op jit(solution)/shard_map/ppermute | solution.py:93
  64.7 33.2 %collective-permute-start.18 = (bf16[64,2176]{1,0:T(8,128)(2,1)S(1)}, bf16[64,2176]{1,0:T(8,128)(2,1)S(1)}, u32[]{:S(2)}, u32[]{:S(2)}) collective-permute-start(bf16[64,2176]{1,0:T(8,128)(2,1)S(1)} %concatenate.40), channel_id=1, source_target_pairs={{0,16},{4,20},{8,24},{12,28},{16,0},{20,4},{24,8},{28,12},{1,17},{... | collective-permute-start | bytes 835592 | tf_op jit(solution)/shard_map/ppermute | solution.py:93
  65.1 39.8 %collective-permute-start.19 = (bf16[64,2176]{1,0:T(8,128)(2,1)S(1)}, bf16[64,2176]{1,0:T(8,128)(2,1)S(1)}, u32[]{:S(2)}, u32[]{:S(2)}) collective-permute-start(bf16[64,2176]{1,0:T(8,128)(2,1)S(1)} %concatenate.40), channel_id=1, source_target_pairs={{0,24},{4,28},{8,0},{12,4},{16,8},{20,12},{24,16},{28,20},{1,25},{... | collective-permute-start | bytes 835592 | tf_op jit(solution)/shard_map/ppermute | solution.py:93
  93.6 13.4 %collective-permute-start.7 = (bf16[2,32,2176]{2,1,0:T(8,128)(2,1)S(1)}, bf16[2,32,2176]{2,1,0:T(8,128)(2,1)S(1)}, u32[]{:S(2)}, u32[]{:S(2)}) collective-permute-start(bf16[2,32,2176]{2,1,0:T(8,128)(2,1)S(1)} %get-tuple-element.42), channel_id=1, source_target_pairs={{0,4},{4,0},{8,12},{12,8},{16,20},{20,16},{24,28},{28,24},{1,5},{5... | collective-permute-start | bytes 835592 | tf_op jit(solution)/shard_map/ppermute | solution.py:107
  104.9 15.7 %collective-permute-start.20 = (bf16[2,32,2176]{2,1,0:T(8,128)(2,1)S(1)}, bf16[2,32,2176]{2,1,0:T(8,128)(2,1)S(1)}, u32[]{:S(2)}, u32[]{:S(2)}) collective-permute-start(bf16[2,32,2176]{2,1,0:T(8,128)(2,1)S(1)} %get-tuple-element.44), channel_id=1, source_target_pairs={{0,4},{4,0},{8,12},{12,8},{16,20},{20,16},{24,28},{28,24},{1,5},{5... | collective-permute-start | bytes 835592 | tf_op jit(solution)/shard_map/ppermute | solution.py:107
  105.5 16.8 %collective-permute-start.22 = (bf16[2,32,2176]{2,1,0:T(8,128)(2,1)S(1)}, bf16[2,32,2176]{2,1,0:T(8,128)(2,1)S(1)}, u32[]{:S(2)}, u32[]{:S(2)}) collective-permute-start(bf16[2,32,2176]{2,1,0:T(8,128)(2,1)S(1)} %get-tuple-element.45), channel_id=1, source_target_pairs={{0,2},{1,3},{2,0},{3,1},{4,6},{5,7},{6,4},{7,5},{8,10},{9,11},{10,... | collective-permute-start | bytes 835592 | tf_op jit(solution)/shard_map/ppermute | solution.py:112
  107.0 12.1 %collective-permute-start.9 = (bf16[2,32,2176]{2,1,0:T(8,128)(2,1)S(1)}, bf16[2,32,2176]{2,1,0:T(8,128)(2,1)S(1)}, u32[]{:S(2)}, u32[]{:S(2)}) collective-permute-start(bf16[2,32,2176]{2,1,0:T(8,128)(2,1)S(1)} %get-tuple-element.43), channel_id=1, source_target_pairs={{0,2},{1,3},{2,0},{3,1},{4,6},{5,7},{6,4},{7,5},{8,10},{9,11},{10,... | collective-permute-start | bytes 835592 | tf_op jit(solution)/shard_map/ppermute | solution.py:112
  119.1 15.6 %collective-permute-start.8 = (bf16[2,2,32,2176]{3,2,1,0:T(8,128)(2,1)S(1)}, bf16[2,2,32,2176]{3,2,1,0:T(8,128)(2,1)S(1)}, u32[]{:S(2)}, u32[]{:S(2)}) collective-permute-start(bf16[2,2,32,2176]{3,2,1,0:T(8,128)(2,1)S(1)} %pad_maximum_fusion.3), channel_id=1, source_target_pairs={{0,2},{1,3},{2,0},{3,1},{4,6},{5,7},{6,4},{7,5},{8,10},{9,11},{10,... | collective-permute-start | bytes 1671176 | tf_op jit(solution)/shard_map/ppermute | solution.py:112
  120.7 46.6 %collective-permute-start.10 = (bf16[2,2,32,2176]{3,2,1,0:T(8,128)(2,1)S(1)}, bf16[2,2,32,2176]{3,2,1,0:T(8,128)(2,1)S(1)}, u32[]{:S(2)}, u32[]{:S(2)}) collective-permute-start(bf16[2,2,32,2176]{3,2,1,0:T(8,128)(2,1)S(1)} %pad_maximum_fusion.4), channel_id=1, source_target_pairs={{0,4},{4,0},{8,12},{12,8},{16,20},{20,16},{24,28},{28,24},{1,5},{5... | collective-permute-start | bytes 1671176 | tf_op jit(solution)/shard_map/ppermute | solution.py:107
  122.3 48.0 %collective-permute-start.21 = (bf16[2,2,32,2176]{3,2,1,0:T(8,128)(2,1)S(1)}, bf16[2,2,32,2176]{3,2,1,0:T(8,128)(2,1)S(1)}, u32[]{:S(2)}, u32[]{:S(2)}) collective-permute-start(bf16[2,2,32,2176]{3,2,1,0:T(8,128)(2,1)S(1)} %pad_maximum_fusion.5), channel_id=1, source_target_pairs={{0,2},{1,3},{2,0},{3,1},{4,6},{5,7},{6,4},{7,5},{8,10},{9,11},{10,... | collective-permute-start | bytes 1671176 | tf_op jit(solution)/shard_map/ppermute | solution.py:112
  134.7 46.3 %collective-permute-start.34 = (bf16[2,1536,256]{2,1,0:T(8,128)(2,1)S(1)}, bf16[2,1536,256]{2,1,0:T(8,128)(2,1)S(1)}, u32[]{:S(2)}, u32[]{:S(2)}) collective-permute-start(bf16[2,1536,256]{2,1,0:T(8,128)(2,1)S(1)} %dynamic-slice_bitcast_fusion), channel_id=1, source_target_pairs={{0,12},{4,8},{8,4},{12,0},{16,28},{20,24},{24,20},{28,16},{1,13},{... | collective-permute-start | bytes 4718600 | tf_op jit(solution)/shard_map/ppermute | solution.py:98
  167.3 11.5 %collective-permute-start.23 = (bf16[2,2,32,2176]{3,2,1,0:T(8,128)(2,1)S(1)}, bf16[2,2,32,2176]{3,2,1,0:T(8,128)(2,1)S(1)}, u32[]{:S(2)}, u32[]{:S(2)}) collective-permute-start(bf16[2,2,32,2176]{3,2,1,0:T(8,128)(2,1)S(1)} %pad_maximum_fusion.6), channel_id=1, source_target_pairs={{0,4},{4,0},{8,12},{12,8},{16,20},{20,16},{24,28},{28,24},{1,5},{5... | collective-permute-start | bytes 1671176 | tf_op jit(solution)/shard_map/ppermute | solution.py:107
  170.3 27.4 %collective-permute-start.11 = (bf16[512,2176]{1,0:T(8,128)(2,1)}, bf16[512,2176]{1,0:T(8,128)(2,1)}, u32[]{:S(2)}, u32[]{:S(2)}) collective-permute-start(bf16[512,2176]{1,0:T(8,128)(2,1)} %pad_maximum_fusion.1.tok_ref), channel_id=1, source_target_pairs={{0,1},{1,0},{2,3},{3,2},{4,5},{5,4},{6,7},{7,6},{8,9},{9,8},{10,11... | collective-permute-start | bytes 6684680 | tf_op jit(solution)/shard_map/ppermute | solution.py:117
  180.3 26.7 %collective-permute-start.24 = (bf16[512,2176]{1,0:T(8,128)(2,1)}, bf16[512,2176]{1,0:T(8,128)(2,1)}, u32[]{:S(2)}, u32[]{:S(2)}) collective-permute-start(bf16[512,2176]{1,0:T(8,128)(2,1)} %pad_maximum_fusion.2.tok_ref), channel_id=1, source_target_pairs={{0,1},{1,0},{2,3},{3,2},{4,5},{5,4},{6,7},{7,6},{8,9},{9,8},{10,11... | collective-permute-start | bytes 6684680 | tf_op jit(solution)/shard_map/ppermute | solution.py:117
  192.9 76.3 %all-to-all-start = ((bf16[4,2,768,256]{3,2,1,0:T(8,128)(2,1)}), bf16[4,2,768,256]{3,2,1,0:T(8,128)(2,1)}, u32[]{:S(2)}, u32[]{:S(2)}) async-start(bf16[4,2,768,256]{3,2,1,0:T(8,128)(2,1)} %bitcast.163), calls=%async_computation | async-start | bytes 6291456 | tf_op jit(solution)/shard_map/all_to_all | solution.py:258
  206.6 29.8 %collective-permute-start.12 = (bf16[512,2048]{1,0:T(8,128)(2,1)}, bf16[512,2048]{1,0:T(8,128)(2,1)}, u32[]{:S(2)}, u32[]{:S(2)}) collective-permute-start(bf16[512,2048]{1,0:T(8,128)(2,1)} %shard_map.177), channel_id=1, source_target_pairs={{0,1},{1,0},{2,3},{3,2},{4,5},{5,4},{6,7},{7,6},{8,9},{9,8},{10,11... | collective-permute-start | bytes 6291464 | tf_op jit(solution)/shard_map/ppermute | solution.py:117
  213.1 29.0 %collective-permute-start.25 = (bf16[512,2048]{1,0:T(8,128)(2,1)}, bf16[512,2048]{1,0:T(8,128)(2,1)}, u32[]{:S(2)}, u32[]{:S(2)}) collective-permute-start(bf16[512,2048]{1,0:T(8,128)(2,1)} %shard_map.179), channel_id=1, source_target_pairs={{0,1},{1,0},{2,3},{3,2},{4,5},{5,4},{6,7},{7,6},{8,9},{9,8},{10,11... | collective-permute-start | bytes 6291464 | tf_op jit(solution)/shard_map/ppermute | solution.py:117
  240.1 38.9 %collective-permute-start.13 = (bf16[2,2,32,2048]{3,2,1,0:T(8,128)(2,1)}, bf16[2,2,32,2048]{3,2,1,0:T(8,128)(2,1)}, u32[]{:S(2)}, u32[]{:S(2)}) collective-permute-start(bf16[2,2,32,2048]{3,2,1,0:T(8,128)(2,1)} %bitcast.44), channel_id=1, source_target_pairs={{0,2},{1,3},{2,0},{3,1},{4,6},{5,7},{6,4},{7,5},{8,10},{9,11},{10,... | collective-permute-start | bytes 1572872 | tf_op jit(solution)/shard_map/ppermute | solution.py:112
  240.6 40.5 %collective-permute-start.15 = (bf16[2,2,32,2048]{3,2,1,0:T(8,128)(2,1)}, bf16[2,2,32,2048]{3,2,1,0:T(8,128)(2,1)}, u32[]{:S(2)}, u32[]{:S(2)}) collective-permute-start(bf16[2,2,32,2048]{3,2,1,0:T(8,128)(2,1)} %bitcast.48), channel_id=1, source_target_pairs={{0,4},{4,0},{8,12},{12,8},{16,20},{20,16},{24,28},{28,24},{1,5},{5... | collective-permute-start | bytes 1572872 | tf_op jit(solution)/shard_map/ppermute | solution.py:107
  245.7 37.3 %collective-permute-start.28 = (bf16[2,2,32,2048]{3,2,1,0:T(8,128)(2,1)}, bf16[2,2,32,2048]{3,2,1,0:T(8,128)(2,1)}, u32[]{:S(2)}, u32[]{:S(2)}) collective-permute-start(bf16[2,2,32,2048]{3,2,1,0:T(8,128)(2,1)} %bitcast.68), channel_id=1, source_target_pairs={{0,4},{4,0},{8,12},{12,8},{16,20},{20,16},{24,28},{28,24},{1,5},{5... | collective-permute-start | bytes 1572872 | tf_op jit(solution)/shard_map/ppermute | solution.py:107
  246.2 39.5 %collective-permute-start.26 = (bf16[2,2,32,2048]{3,2,1,0:T(8,128)(2,1)}, bf16[2,2,32,2048]{3,2,1,0:T(8,128)(2,1)}, u32[]{:S(2)}, u32[]{:S(2)}) collective-permute-start(bf16[2,2,32,2048]{3,2,1,0:T(8,128)(2,1)} %bitcast.64), channel_id=1, source_target_pairs={{0,2},{1,3},{2,0},{3,1},{4,6},{5,7},{6,4},{7,5},{8,10},{9,11},{10,... | collective-permute-start | bytes 1572872 | tf_op jit(solution)/shard_map/ppermute | solution.py:112
  269.2 87.8 %all-to-all-start.1 = ((bf16[4,2,768,256]{3,2,1,0:T(8,128)(2,1)}), bf16[4,2,768,256]{3,2,1,0:T(8,128)(2,1)}, u32[]{:S(2)}, u32[]{:S(2)}) async-start(bf16[4,2,768,256]{3,2,1,0:T(8,128)(2,1)} %bitcast.162), calls=%async_computation.1 | async-start | bytes 6291456 | tf_op jit(solution)/shard_map/all_to_all | solution.py:258
  276.0 83.9 %collective-permute-start.35 = (bf16[2,1,768,256]{3,2,1,0:T(8,128)(2,1)}, bf16[2,1,768,256]{3,2,1,0:T(8,128)(2,1)}, u32[]{:S(2)}, u32[]{:S(2)}) collective-permute-start(bf16[2,1,768,256]{3,2,1,0:T(8,128)(2,1)} %constant_dynamic-slice_fusion.1), channel_id=1, source_target_pairs={{0,4},{4,0},{8,12},{12,8},{16,20},{20,16},{24,28},{28,24},{1,5},{5... | collective-permute-start | bytes 2359304 | tf_op jit(solution)/shard_map/ppermute | solution.py:98
  279.0 5.2 %copy-start.10 = (bf16[2,2,2,768,256]{4,3,2,1,0:T(8,128)(2,1)}, bf16[2,2,2,768,256]{4,3,2,1,0:T(8,128)(2,1)S(1)}, u32[]{:S(2)}) copy-start(bf16[2,2,2,768,256]{4,3,2,1,0:T(8,128)(2,1)S(1)} %bitcast_dynamic-update-slice_fusion.3) | copy-start | bytes 9437188
  280.6 21.7 %collective-permute-start.14 = (bf16[2,32,2048]{2,1,0:T(8,128)(2,1)S(1)}, bf16[2,32,2048]{2,1,0:T(8,128)(2,1)S(1)}, u32[]{:S(2)}, u32[]{:S(2)}) collective-permute-start(bf16[2,32,2048]{2,1,0:T(8,128)(2,1)S(1)} %slice_bitcast_fusion.6), channel_id=1, source_target_pairs={{0,4},{4,0},{8,12},{12,8},{16,20},{20,16},{24,28},{28,24},{1,5},{5... | collective-permute-start | bytes 786440 | tf_op jit(solution)/shard_map/ppermute | solution.py:107
  282.4 19.9 %collective-permute-start.16 = (bf16[2,32,2048]{2,1,0:T(8,128)(2,1)S(1)}, bf16[2,32,2048]{2,1,0:T(8,128)(2,1)S(1)}, u32[]{:S(2)}, u32[]{:S(2)}) collective-permute-start(bf16[2,32,2048]{2,1,0:T(8,128)(2,1)S(1)} %slice_bitcast_fusion.4), channel_id=1, source_target_pairs={{0,2},{1,3},{2,0},{3,1},{4,6},{5,7},{6,4},{7,5},{8,10},{9,11},{10,... | collective-permute-start | bytes 786440 | tf_op jit(solution)/shard_map/ppermute | solution.py:112
  284.2 22.1 %collective-permute-start.29 = (bf16[2,32,2048]{2,1,0:T(8,128)(2,1)S(1)}, bf16[2,32,2048]{2,1,0:T(8,128)(2,1)S(1)}, u32[]{:S(2)}, u32[]{:S(2)}) collective-permute-start(bf16[2,32,2048]{2,1,0:T(8,128)(2,1)S(1)} %slice_bitcast_fusion), channel_id=1, source_target_pairs={{0,2},{1,3},{2,0},{3,1},{4,6},{5,7},{6,4},{7,5},{8,10},{9,11},{10,... | collective-permute-start | bytes 786440 | tf_op jit(solution)/shard_map/ppermute | solution.py:112
  286.9 19.6 %collective-permute-start.27 = (bf16[2,32,2048]{2,1,0:T(8,128)(2,1)S(1)}, bf16[2,32,2048]{2,1,0:T(8,128)(2,1)S(1)}, u32[]{:S(2)}, u32[]{:S(2)}) collective-permute-start(bf16[2,32,2048]{2,1,0:T(8,128)(2,1)S(1)} %slice_bitcast_fusion.2), channel_id=1, source_target_pairs={{0,4},{4,0},{8,12},{12,8},{16,20},{20,16},{24,28},{28,24},{1,5},{5... | collective-permute-start | bytes 786440 | tf_op jit(solution)/shard_map/ppermute | solution.py:107
  302.4 59.6 %collective-permute-start.17 = (bf16[64,2048]{1,0:T(8,128)(2,1)S(1)}, bf16[64,2048]{1,0:T(8,128)(2,1)}, u32[]{:S(2)}, u32[]{:S(2)}) collective-permute-start(bf16[64,2048]{1,0:T(8,128)(2,1)S(1)} %fusion.37), channel_id=1, source_target_pairs={{0,24},{4,28},{8,0},{12,4},{16,8},{20,12},{24,16},{28,20},{1,25},{... | collective-permute-start | bytes 786440 | tf_op jit(solution)/shard_map/ppermute | solution.py:93
  307.5 59.7 %collective-permute-start.30 = (bf16[64,2048]{1,0:T(8,128)(2,1)}, bf16[64,2048]{1,0:T(8,128)(2,1)}, u32[]{:S(2)}, u32[]{:S(2)}) collective-permute-start(bf16[64,2048]{1,0:T(8,128)(2,1)} %get-tuple-element.46), channel_id=1, source_target_pairs={{0,16},{4,20},{8,24},{12,28},{16,0},{20,4},{24,8},{28,12},{1,17},{... | collective-permute-start | bytes 786440 | tf_op jit(solution)/shard_map/ppermute | solution.py:93
  310.1 57.2 %collective-permute-start.31 = (bf16[64,2048]{1,0:T(8,128)(2,1)}, bf16[64,2048]{1,0:T(8,128)(2,1)}, u32[]{:S(2)}, u32[]{:S(2)}) collective-permute-start(bf16[64,2048]{1,0:T(8,128)(2,1)} %get-tuple-element.47), channel_id=1, source_target_pairs={{0,8},{4,12},{8,16},{12,20},{16,24},{20,28},{24,0},{28,4},{1,9},{5... | collective-permute-start | bytes 786440 | tf_op jit(solution)/shard_map/ppermute | solution.py:93
  358.2 17.6 %collective-permute-start.36 = (bf16[2,1,768,256]{3,2,1,0:T(8,128)(2,1)S(1)}, bf16[2,1,768,256]{3,2,1,0:T(8,128)(2,1)S(1)}, u32[]{:S(2)}, u32[]{:S(2)}) collective-permute-start(bf16[2,1,768,256]{3,2,1,0:T(8,128)(2,1)S(1)} %constant_dynamic-slice_fusion), channel_id=1, source_target_pairs={{0,4},{4,0},{8,12},{12,8},{16,20},{20,16},{24,28},{28,24},{1,5},{5... | collective-permute-start | bytes 2359304 | tf_op jit(solution)/shard_map/ppermute | solution.py:98
  359.8 16.9 %copy-start.1 = (bf16[512,2048]{1,0:T(8,128)(2,1)S(1)}, bf16[512,2048]{1,0:T(8,128)(2,1)}, u32[]{:S(2)}) copy-start(bf16[512,2048]{1,0:T(8,128)(2,1)} %param.27) | copy-start | bytes 6291460
  (14 other events, 35.3 us)
